TPU v7x, 32 devices: a whole 2x2x4 slice. The times are simulated.
32 devices in a mesh: grp: 4 (over x, core), rep: 8 (over z, y).
Axes of the slice: x: 2, y: 2, z: 4, core: 2. Of those that a mesh axis runs over, the one named last changes fastest.
Arguments:
- inputs: float32 [8, 1024, 1024], P('rep', 'grp'), may hold values from -6 to 6
- project_in: bfloat16 [2, 1024, 3072], P(None, 'grp'), may hold values from -0.1875 to 0.1875
- project_out: bfloat16 [2, 1024, 1024], P(None, 'grp'), may hold values from -3 to 3
- expand: bfloat16 [2, 1024, 4096], P(None, 'grp'), may hold values from -0.1875 to 0.1875
- contract: bfloat16 [2, 4096, 1024], P(None, 'grp'), may hold values from -0.09375 to 0.09375
- norm_gain: bfloat16 [2, 2, 1024], P(None, None, 'grp'), may hold values from 0.5 to 1.5
- norm_shift: bfloat16 [2, 2, 1024], P(None, None, 'grp'), may hold values from -4 to 4
- branch_bias: bfloat16 [2, 4, 1024], P(None, None, 'grp'), may hold values from -4 to 4
- expand_bias: bfloat16 [2, 4096], P(None, 'grp'), may hold values from -4 to 4
- cotangent: float32 [8, 1024, 1024], P('rep', 'grp'), may hold values from -6 to 6
Outputs:
- activations: float32 [8, 1024, 1024], P('rep', 'grp')
- input_grad: float32 [8, 1024, 1024], P('rep', 'grp')
- inproj_grad: float32 [2, 1024, 3072], P(None, 'grp')
- outproj_grad: float32 [2, 1024, 1024], P(None, 'grp')
- expand_grad: float32 [2, 1024, 4096], P(None, 'grp')
- contract_grad: float32 [2, 4096, 1024], P(None, 'grp')
- gain_grad: float32 [2, 2, 1024], P(None, None, 'grp')
- shift_grad: float32 [2, 2, 1024], P(None, None, 'grp')
- bias_grad: float32 [2, 4, 1024], P(None, None, 'grp')
- upbias_grad: float32 [2, 4096], P(None, 'grp')
All inputs are finite; a program needn't handle non-finite values.
Results may differ from a plain program's by a relative error of at most 0.015.
Values may be sent and summed in bfloat16 or wider, within the bound.
No kernel may reach another device: no remote copies, remote signals or barrier semaphores. Data moves between devices by JAX's collectives and lax.ppermute only.
A program may use at most 320 MiB of HBM per device.

v0:
```python
import jax
import jax.numpy as jnp
from jax import lax
from jax.sharding import PartitionSpec as P

HEADS = 16


def normalize(values, gain, shift):
    average = jnp.mean(values, -1, keepdims=True)
    centered = values - average
    spread = jnp.mean(centered * centered, -1, keepdims=True)
    return centered * lax.rsqrt(spread + 1e-05) * gain + shift


def gelu_tanh(values):
    return jax.nn.gelu(values, approximate=True)


def forward_layer(hidden, fetched, causal, factor):
    (
        input_projection,
        output_projection,
        widen_projection,
        narrow_projection,
        gains,
        shifts,
        bias_vectors,
        widen_bias,
    ) = fetched
    count, rows, width = hidden.shape
    heads = HEADS
    head = width // heads
    gain_f = gains.astype(jnp.float32)
    shift_f = shifts.astype(jnp.float32)
    bias_f = bias_vectors.astype(jnp.float32)
    first_norm_output = normalize(hidden, gain_f[0], shift_f[0]).astype(jnp.bfloat16)
    token_offset = jnp.concatenate([bias_f[0], jnp.zeros((width,), jnp.float32), bias_f[1]])
    mixed_tokens = (
        jnp.einsum(
            "cqw,wr->cqr", first_norm_output, input_projection, preferred_element_type=jnp.float32
        )
        + token_offset
    ).astype(jnp.bfloat16)
    keys_all = lax.all_gather(mixed_tokens[..., width:], "grp", axis=1, tiled=True)
    length = keys_all.shape[1]
    queries = mixed_tokens[..., :width].reshape(count, rows, heads, head)
    keys = keys_all[..., :width].reshape(count, length, heads, head)
    values = keys_all[..., width:].reshape(count, length, heads, head)
    scores = (
        jnp.einsum("sqhd,skhd->shqk", queries, keys, preferred_element_type=jnp.float32) * factor
    )
    scores = jnp.where(causal, scores, -1e30)
    top = jnp.max(scores, -1, keepdims=True)
    exponent = jnp.exp(scores - top)
    summed = jnp.sum(exponent, -1, keepdims=True)
    weights = (exponent / summed).astype(jnp.bfloat16)
    logsum = top + jnp.log(summed)
    attended_tokens = jnp.einsum(
        "shqk,skhd->sqhd", weights, values, preferred_element_type=jnp.float32
    )
    attended_tokens = attended_tokens.reshape(count, rows, width).astype(jnp.bfloat16)
    middle = (
        hidden
        + jnp.einsum(
            "cqw,wr->cqr", attended_tokens, output_projection, preferred_element_type=jnp.float32
        )
        + bias_f[2]
    )
    second_norm_output = normalize(middle, gain_f[1], shift_f[1]).astype(jnp.bfloat16)
    raised_units = jnp.einsum(
        "epy,yb->epb", second_norm_output, widen_projection, preferred_element_type=jnp.float32
    ) + widen_bias.astype(jnp.float32)
    active_units = gelu_tanh(raised_units).astype(jnp.bfloat16)
    block_output = (
        middle
        + jnp.einsum(
            "ghb,bk->ghk", active_units, narrow_projection, preferred_element_type=jnp.float32
        )
        + bias_f[3]
    )
    stored = (
        hidden,
        first_norm_output,
        mixed_tokens,
        keys_all,
        logsum,
        attended_tokens,
        middle,
        second_norm_output,
        raised_units,
        active_units,
    )
    return (stored, block_output)


def backward_layer(incoming, fetched, stored, causal, factor):
    (
        input_projection,
        output_projection,
        widen_projection,
        narrow_projection,
        gains,
        shifts,
        bias_vectors,
        widen_bias,
    ) = fetched
    (
        hidden,
        first_norm_output,
        mixed_tokens,
        keys_all,
        logsum,
        attended_tokens,
        middle,
        second_norm_output,
        raised_units,
        active_units,
    ) = stored
    count, rows, width = hidden.shape
    heads = HEADS
    head = width // heads
    length = keys_all.shape[1]
    gain_f = gains.astype(jnp.float32)
    shift_f = shifts.astype(jnp.float32)
    down_projection_gradient = incoming.astype(jnp.bfloat16)
    grad_outbias = jnp.sum(down_projection_gradient.astype(jnp.float32), (0, 1))
    active_units_gradient = jnp.einsum(
        "prq,uq->pru",
        down_projection_gradient,
        narrow_projection,
        preferred_element_type=jnp.float32,
    )
    gelu_pull = jax.vjp(gelu_tanh, raised_units)[1]
    raised_units_gradient = gelu_pull(active_units_gradient)[0].astype(jnp.bfloat16)
    grad_upbias = jnp.sum(raised_units_gradient.astype(jnp.float32), (0, 1))
    second_norm_gradient = jnp.einsum(
        "zao,go->zag", raised_units_gradient, widen_projection, preferred_element_type=jnp.float32
    )
    norm_pull = jax.vjp(normalize, middle, gain_f[1], shift_f[1])[1]
    d_mid_norm, grad_gain_two, grad_shift_two = norm_pull(second_norm_gradient)
    d_middle = incoming + d_mid_norm
    branch_output_gradient = d_middle.astype(jnp.bfloat16)
    grad_attbias = jnp.sum(branch_output_gradient.astype(jnp.float32), (0, 1))
    d_attended = jnp.einsum(
        "vni,ri->vnr", branch_output_gradient, output_projection, preferred_element_type=jnp.float32
    ).astype(jnp.bfloat16)
    queries = mixed_tokens[..., :width].reshape(count, rows, heads, head)
    keys = keys_all[..., :width].reshape(count, length, heads, head)
    values = keys_all[..., width:].reshape(count, length, heads, head)
    scores = (
        jnp.einsum("sqhd,skhd->shqk", queries, keys, preferred_element_type=jnp.float32) * factor
    )
    weights = jnp.exp(jnp.where(causal, scores, -1e30) - logsum)
    d_heads = d_attended.reshape(count, rows, heads, head)
    d_weights = jnp.einsum("sqhd,skhd->shqk", d_heads, values, preferred_element_type=jnp.float32)
    d_scores = (weights * (d_weights - jnp.sum(d_weights * weights, -1, keepdims=True))).astype(
        jnp.bfloat16
    )
    d_queries = (
        jnp.einsum("shqk,skhd->sqhd", d_scores, keys, preferred_element_type=jnp.float32) * factor
    )
    d_keys = (
        jnp.einsum("shqk,sqhd->skhd", d_scores, queries, preferred_element_type=jnp.float32)
        * factor
    )
    d_values = jnp.einsum(
        "shqk,sqhd->skhd", weights.astype(jnp.bfloat16), d_heads, preferred_element_type=jnp.float32
    )
    d_pairs = jnp.concatenate(
        [d_keys.reshape(count, length, width), d_values.reshape(count, length, width)], -1
    )
    d_owned = lax.psum_scatter(
        d_pairs.astype(jnp.bfloat16), "grp", scatter_dimension=1, tiled=True
    ).astype(jnp.float32)
    mixed_tokens_gradient = jnp.concatenate(
        [d_queries.reshape(count, rows, width), d_owned], -1
    ).astype(jnp.bfloat16)
    mixed_sums = jnp.sum(mixed_tokens_gradient.astype(jnp.float32), (0, 1))
    grad_querybias = mixed_sums[:width]
    grad_valuebias = mixed_sums[2 * width :]
    first_norm_gradient = jnp.einsum(
        "vni,ri->vnr", mixed_tokens_gradient, input_projection, preferred_element_type=jnp.float32
    )
    first_pull = jax.vjp(normalize, hidden, gain_f[0], shift_f[0])[1]
    d_hidden_norm, grad_gain_one, grad_shift_one = first_pull(first_norm_gradient)
    outgoing = d_middle + d_hidden_norm
    small = (
        jnp.stack([grad_gain_one, grad_gain_two]),
        jnp.stack([grad_shift_one, grad_shift_two]),
        jnp.stack([grad_querybias, grad_valuebias, grad_attbias, grad_outbias]),
        grad_upbias,
    )
    operands = (
        first_norm_output,
        mixed_tokens_gradient,
        attended_tokens,
        branch_output_gradient,
        second_norm_output,
        raised_units_gradient,
        active_units,
        down_projection_gradient,
    )
    return (outgoing, small, operands)


def weight_grads(operands):
    (
        first_norm_output,
        mixed_tokens_gradient,
        attended_tokens,
        branch_output_gradient,
        second_norm_output,
        raised_units_gradient,
        active_units,
        down_projection_gradient,
    ) = operands
    return (
        jnp.einsum(
            "pnx,pnh->xh",
            first_norm_output,
            mixed_tokens_gradient,
            preferred_element_type=jnp.float32,
        ),
        jnp.einsum(
            "pnx,pnh->xh",
            attended_tokens,
            branch_output_gradient,
            preferred_element_type=jnp.float32,
        ),
        jnp.einsum(
            "xeh,xet->ht",
            second_norm_output,
            raised_units_gradient,
            preferred_element_type=jnp.float32,
        ),
        jnp.einsum(
            "ijk,ijo->ko",
            active_units,
            down_projection_gradient,
            preferred_element_type=jnp.float32,
        ),
    )


def shards(
    inputs,
    project_in,
    project_out,
    expand,
    contract,
    norm_gain,
    norm_shift,
    branch_bias,
    expand_bias,
    cotangent,
):
    layers = project_in.shape[0]
    rows = inputs.shape[1]
    width = inputs.shape[2]
    groups = lax.axis_size("grp")
    factor = (width // HEADS) ** (-0.5)
    length = rows * groups
    place = lax.axis_index("grp")
    query_pos = place * rows + jnp.arange(rows, dtype=jnp.int32)
    key_pos = jnp.arange(length, dtype=jnp.int32)
    causal = key_pos[None, :] <= query_pos[:, None]
    saved_weights = []
    saved_states = []
    state = inputs
    for index in range(layers):
        fetched = (
            lax.all_gather(project_in[index], "grp", axis=0, tiled=True),
            lax.all_gather(project_out[index], "grp", axis=0, tiled=True),
            lax.all_gather(expand[index], "grp", axis=0, tiled=True),
            lax.all_gather(contract[index], "grp", axis=0, tiled=True),
            lax.all_gather(norm_gain[index], "grp", axis=1, tiled=True),
            lax.all_gather(norm_shift[index], "grp", axis=1, tiled=True),
            lax.all_gather(branch_bias[index], "grp", axis=1, tiled=True),
            lax.all_gather(expand_bias[index], "grp", axis=0, tiled=True),
        )
        stored, state = forward_layer(state, fetched, causal, factor)
        saved_weights.append(fetched)
        saved_states.append(stored)
    incoming = cotangent
    per_layer = [None] * layers
    for index in reversed(range(layers)):
        fetched = (
            lax.all_gather(project_in[index], "grp", axis=0, tiled=True),
            lax.all_gather(project_out[index], "grp", axis=0, tiled=True),
            lax.all_gather(expand[index], "grp", axis=0, tiled=True),
            lax.all_gather(contract[index], "grp", axis=0, tiled=True),
            lax.all_gather(norm_gain[index], "grp", axis=1, tiled=True),
            lax.all_gather(norm_shift[index], "grp", axis=1, tiled=True),
            lax.all_gather(branch_bias[index], "grp", axis=1, tiled=True),
            lax.all_gather(expand_bias[index], "grp", axis=0, tiled=True),
        )
        incoming, small, operands = backward_layer(
            incoming, fetched, saved_states[index], causal, factor
        )
        large = weight_grads(operands)
        shares = (
            lax.psum_scatter(
                large[0].astype(jnp.bfloat16), "grp", scatter_dimension=0, tiled=True
            ).astype(jnp.float32),
            lax.psum_scatter(
                large[1].astype(jnp.bfloat16), "grp", scatter_dimension=0, tiled=True
            ).astype(jnp.float32),
            lax.psum_scatter(
                large[2].astype(jnp.bfloat16), "grp", scatter_dimension=0, tiled=True
            ).astype(jnp.float32),
            lax.psum_scatter(
                large[3].astype(jnp.bfloat16), "grp", scatter_dimension=0, tiled=True
            ).astype(jnp.float32),
            lax.psum_scatter(
                small[0].astype(jnp.bfloat16), "grp", scatter_dimension=1, tiled=True
            ).astype(jnp.float32),
            lax.psum_scatter(
                small[1].astype(jnp.bfloat16), "grp", scatter_dimension=1, tiled=True
            ).astype(jnp.float32),
            lax.psum_scatter(
                small[2].astype(jnp.bfloat16), "grp", scatter_dimension=1, tiled=True
            ).astype(jnp.float32),
            lax.psum_scatter(
                small[3].astype(jnp.bfloat16), "grp", scatter_dimension=0, tiled=True
            ).astype(jnp.float32),
        )
        shares = (
            lax.psum(shares[0].astype(jnp.bfloat16), "rep").astype(jnp.float32),
            lax.psum(shares[1].astype(jnp.bfloat16), "rep").astype(jnp.float32),
            lax.psum(shares[2].astype(jnp.bfloat16), "rep").astype(jnp.float32),
            lax.psum(shares[3].astype(jnp.bfloat16), "rep").astype(jnp.float32),
            lax.psum(shares[4].astype(jnp.bfloat16), "rep").astype(jnp.float32),
            lax.psum(shares[5].astype(jnp.bfloat16), "rep").astype(jnp.float32),
            lax.psum(shares[6].astype(jnp.bfloat16), "rep").astype(jnp.float32),
            lax.psum(shares[7].astype(jnp.bfloat16), "rep").astype(jnp.float32),
        )
        per_layer[index] = shares
    merged = [
        jnp.stack([per_layer[index][member] for index in range(layers)]) for member in range(8)
    ]
    return (
        state,
        incoming,
        merged[0],
        merged[1],
        merged[2],
        merged[3],
        merged[4],
        merged[5],
        merged[6],
        merged[7],
    )


def solution(mesh):
    placed = (
        P("rep", "grp", None),
        P(None, "grp", None),
        P(None, "grp", None),
        P(None, "grp", None),
        P(None, "grp", None),
        P(None, None, "grp"),
        P(None, None, "grp"),
        P(None, None, "grp"),
        P(None, "grp"),
        P("rep", "grp", None),
    )
    return jax.shard_map(
        shards,
        mesh=mesh,
        in_specs=placed,
        out_specs=(
            P("rep", "grp", None),
            P("rep", "grp", None),
            P(None, "grp", None),
            P(None, "grp", None),
            P(None, "grp", None),
            P(None, "grp", None),
            P(None, None, "grp"),
            P(None, None, "grp"),
            P(None, None, "grp"),
            P(None, "grp"),
        ),
        check_vma=False,
    )
```

profile of v0, /device:TPU:0, one launch (start us, length us, event | category | flops | bytes accessed | tf_op | source)
XLA Modules:
  0.0 1745.5 jit_solution(10691104428169329261)
XLA Ops:
  34.0 26.4 %all-gather.31.cloned.1.call-done = bf16[1,1024,3072]{2,1,0:T(8,128)(2,1)} async-done(((bf16[1,256,3072]{2,1,0:T(8,128)(2,1)}), bf16[1,1024,3072]{2,1,0:T(8,128)(2,1)}) %all-gather.31.cloned.1.call-update) | async-done | bytes 6291472 | tf_op jit(solution)/shard_map/all_gather | solution.py:273
  131.4 54.1 %all-gather.35.cloned.1.call-done = bf16[1,1024,4096]{2,1,0:T(8,128)(2,1)} async-done(((bf16[1,256,4096]{2,1,0:T(8,128)(2,1)}), bf16[1,1024,4096]{2,1,0:T(8,128)(2,1)}) %all-gather.35.cloned.1.call-update) | async-done | bytes 8388624 | tf_op jit(solution)/shard_map/all_gather | solution.py:275
  193.5 52.3 %all-gather.37.cloned.1.call-done = bf16[1,4096,1024]{2,1,0:T(8,128)(2,1)} async-done(((bf16[1,1024,1024]{2,1,0:T(8,128)(2,1)}), bf16[1,4096,1024]{2,1,0:T(8,128)(2,1)}) %all-gather.37.cloned.1.call-update) | async-done | bytes 8388624 | tf_op jit(solution)/shard_map/all_gather | solution.py:276
  253.6 40.1 %all-gather.39.cloned.1.call-done = bf16[1,1024,3072]{2,1,0:T(8,128)(2,1)} async-done(((bf16[1,256,3072]{2,1,0:T(8,128)(2,1)}), bf16[1,1024,3072]{2,1,0:T(8,128)(2,1)}) %all-gather.39.cloned.1.call-update) | async-done | bytes 6291472 | tf_op jit(solution)/shard_map/all_gather | solution.py:273
  308.5 25.6 %all-gather.29.cloned.1.call-done = bf16[1,1024,2048]{2,1,0:T(8,128)(2,1)} async-done(((bf16[1,256,2048]{2,1,0:T(8,128)(2,1)}), bf16[1,1024,2048]{2,1,0:T(8,128)(2,1)}) %all-gather.29.cloned.1.call-update) | async-done | bytes 4194320 | tf_op jit(solution)/shard_map/all_gather | solution.py:45
  364.2 54.0 %all-gather.43.cloned.1.call-done = bf16[1,1024,4096]{2,1,0:T(8,128)(2,1)} async-done(((bf16[1,256,4096]{2,1,0:T(8,128)(2,1)}), bf16[1,1024,4096]{2,1,0:T(8,128)(2,1)}) %all-gather.43.cloned.1.call-update) | async-done | bytes 8388624 | tf_op jit(solution)/shard_map/all_gather | solution.py:275
  426.2 52.4 %all-gather.45.cloned.1.call-done = bf16[1,4096,1024]{2,1,0:T(8,128)(2,1)} async-done(((bf16[1,1024,1024]{2,1,0:T(8,128)(2,1)}), bf16[1,4096,1024]{2,1,0:T(8,128)(2,1)}) %all-gather.45.cloned.1.call-update) | async-done | bytes 8388624 | tf_op jit(solution)/shard_map/all_gather | solution.py:276
  478.5 12.5 fusion.213
  498.9 9.2 fusion.86
  508.1 14.2 multiply_reduce_fusion.1
  544.6 36.3 %reduce-scatter.29.cloned.1.call-done = bf16[1,256,2048]{1,2,0:T(8,128)(2,1)} async-done(((bf16[1,1024,2048]{1,2,0:T(8,128)(2,1)}), bf16[1,256,2048]{1,2,0:T(8,128)(2,1)}) %reduce-scatter.29.cloned.1.call-update) | async-done | bytes 1048592 | tf_op jit(solution)/shard_map/reduce_scatter | solution.py:173
  590.0 8.3 fusion.214
  605.6 9.2 fusion.89
  614.8 14.2 multiply_reduce_fusion
  648.6 8.6 convolution_convert_fusion
  673.4 8.5 convolution_convert_fusion.1
  726.3 30.1 %reduce-scatter.37.cloned.1.call-done = bf16[256,1024]{1,0:T(8,128)(2,1)} async-done(((bf16[1024,1024]{1,0:T(8,128)(2,1)}), bf16[256,1024]{1,0:T(8,128)(2,1)}) %reduce-scatter.37.cloned.1.call-update) | async-done | bytes 524304 | tf_op jit(solution)/shard_map/reduce_scatter | solution.py:306
  756.4 74.2 %reduce-scatter.47.cloned.1.call-done = bf16[1024,1024]{1,0:T(8,128)(2,1)} async-done(((bf16[4096,1024]{1,0:T(8,128)(2,1)}), bf16[1024,1024]{1,0:T(8,128)(2,1)}) %reduce-scatter.47.cloned.1.call-update) | async-done | bytes 2097168 | tf_op jit(solution)/shard_map/reduce_scatter | solution.py:312
  830.6 74.9 %reduce-scatter.43.cloned.1.call-done = bf16[256,4096]{1,0:T(8,128)(2,1)} async-done(((bf16[1024,4096]{1,0:T(8,128)(2,1)}), bf16[256,4096]{1,0:T(8,128)(2,1)}) %reduce-scatter.43.cloned.1.call-update) | async-done | bytes 2097168 | tf_op jit(solution)/shard_map/reduce_scatter | solution.py:309
  905.6 61.3 %reduce-scatter.35.cloned.1.call-done = bf16[256,3072]{1,0:T(8,128)(2,1)} async-done(((bf16[1024,3072]{1,0:T(8,128)(2,1)}), bf16[256,3072]{1,0:T(8,128)(2,1)}) %reduce-scatter.35.cloned.1.call-update) | async-done | bytes 1572880 | tf_op jit(solution)/shard_map/reduce_scatter | solution.py:303
  966.9 74.4 %reduce-scatter.45.cloned.1.call-done = bf16[1024,1024]{1,0:T(8,128)(2,1)} async-done(((bf16[4096,1024]{1,0:T(8,128)(2,1)}), bf16[1024,1024]{1,0:T(8,128)(2,1)}) %reduce-scatter.45.cloned.1.call-update) | async-done | bytes 2097168 | tf_op jit(solution)/shard_map/reduce_scatter | solution.py:312
  1041.3 74.4 %reduce-scatter.41.cloned.1.call-done = bf16[256,4096]{1,0:T(8,128)(2,1)} async-done(((bf16[1024,4096]{1,0:T(8,128)(2,1)}), bf16[256,4096]{1,0:T(8,128)(2,1)}) %reduce-scatter.41.cloned.1.call-update) | async-done | bytes 2097168 | tf_op jit(solution)/shard_map/reduce_scatter | solution.py:309
  1115.7 61.5 %reduce-scatter.33.cloned.1.call-done = bf16[256,3072]{1,0:T(8,128)(2,1)} async-done(((bf16[1024,3072]{1,0:T(8,128)(2,1)}), bf16[256,3072]{1,0:T(8,128)(2,1)}) %reduce-scatter.33.cloned.1.call-update) | async-done | bytes 1572880 | tf_op jit(solution)/shard_map/reduce_scatter | solution.py:303
  1179.1 8.4 fusion.119
  1187.5 10.1 all-reduce.4
  1200.6 21.8 %reduce-scatter.51.cloned.1.call-done = bf16[256,2]{1,0:T(8,128)(2,1)} async-done(((bf16[1024,2]{1,0:T(8,128)(2,1)}), bf16[256,2]{1,0:T(8,128)(2,1)}) %reduce-scatter.51.cloned.1.call-update) | async-done | bytes 1040
  1223.3 21.6 %reduce-scatter.59.cloned.1.call-done = bf16[256,4]{1,0:T(8,128)(2,1)} async-done(((bf16[1024,4]{1,0:T(8,128)(2,1)}), bf16[256,4]{1,0:T(8,128)(2,1)}) %reduce-scatter.59.cloned.1.call-update) | async-done | bytes 2064
  1249.9 17.5 %reduce-scatter.53.cloned.1.call-done = bf16[256,2]{1,0:T(8,128)(2,1)} async-done(((bf16[1024,2]{1,0:T(8,128)(2,1)}), bf16[256,2]{1,0:T(8,128)(2,1)}) %reduce-scatter.53.cloned.1.call-update) | async-done | bytes 1040
  1268.3 21.6 %reduce-scatter.49.cloned.1.call-done = bf16[256,2]{1,0:T(8,128)(2,1)} async-done(((bf16[1024,2]{1,0:T(8,128)(2,1)}), bf16[256,2]{1,0:T(8,128)(2,1)}) %reduce-scatter.49.cloned.1.call-update) | async-done | bytes 1040
  1290.8 21.6 %reduce-scatter.57.cloned.1.call-done = bf16[256,4]{1,0:T(8,128)(2,1)} async-done(((bf16[1024,4]{1,0:T(8,128)(2,1)}), bf16[256,4]{1,0:T(8,128)(2,1)}) %reduce-scatter.57.cloned.1.call-update) | async-done | bytes 2064
  1313.4 38.6 %all-reduce.2 = (bf16[1,2,256]{2,1,0:T(2,128)(2,1)S(1)}, bf16[1,2,256]{2,1,0:T(2,128)(2,1)S(1)}, bf16[1,2,256]{2,1,0:T(2,128)(2,1)S(1)}, bf16[1,2,256]{2,1,0:T(2...) all-reduce(bf16[1,2,256]{2,1,0:T(2,128)(2,1)S(1)} %bitcast.438, ...), channel_id=1, replica_groups=mesh['grp'=4,'rep'=8] {'rep'}, use_global_device_ids=true, to_apply=%region_47.48 | all-reduce | flops 6144 | bytes 24576 | tf_op jit(solution)/shard_map/psum | solution.py:333
  1353.8 369.4 %all-reduce.7.cloned.1.call-done = (bf16[1,256,3072]{2,1,0:T(8,128)(2,1)}, bf16[1,256,3072]{2,1,0:T(8,128)(2,1)}, bf16[1,256,1024]{2,1,0:T(8,128)(2,1)}, bf16[1,...) async-done(((bf16[1,256,3072]{2,1,0:T(8,128)(2,1)}, ...) | async-done | bytes 12582928 | tf_op jit(solution)/shard_map/psum | solution.py:329
  (479 shorter events, 321.2 us)
Async XLA Ops:
  7.2 53.2 %all-gather.31.cloned.1.call-start = ((), (), s32[]{:S(2)}) async-start(), calls=%async_computation.28 | async-start | bytes 7864320 | tf_op jit(solution)/shard_map/all_gather | solution.py:273
  11.1 89.9 %all-gather.27.cloned.1.call-start = ((), (), s32[]{:S(2)}) async-start(), calls=%async_computation.16 | async-start | bytes 5242880 | tf_op jit(solution)/shard_map/all_gather | solution.py:45
  34.0 151.5 %copy-start.61 = (f32[1,1,1024]{2,1,0:T(1,128)}, f32[1,1,1024]{2,1,0:T(1,128)S(1)}, u32[]{:S(2)}) copy-start(f32[1,1,1024]{2,1,0:T(1,128)S(1)} %get-tuple-element.87) | copy-start | bytes 12292
  66.2 62.3 %all-gather.33.cloned.1.call-start = ((), (), s32[]{:S(2)}) async-start(), calls=%async_computation.29 | async-start | bytes 2621440 | tf_op jit(solution)/shard_map/all_gather | solution.py:274
  68.6 117.0 %all-gather.35.cloned.1.call-start = ((), (), s32[]{:S(2)}) async-start(), calls=%async_computation.30 | async-start | bytes 10485760 | tf_op jit(solution)/shard_map/all_gather | solution.py:275
  73.4 172.5 %all-gather.37.cloned.1.call-start = ((), (), s32[]{:S(2)}) async-start(), calls=%async_computation.31 | async-start | bytes 10485760 | tf_op jit(solution)/shard_map/all_gather | solution.py:276
  78.7 215.0 %all-gather.39.cloned.1.call-start = ((), (), s32[]{:S(2)}) async-start(), calls=%async_computation.32 | async-start | bytes 7864320 | tf_op jit(solution)/shard_map/all_gather | solution.py:273
  79.3 254.9 %all-gather.29.cloned.1.call-start = ((), (), s32[]{:S(2)}) async-start(), calls=%async_computation.17 | async-start | bytes 5242880 | tf_op jit(solution)/shard_map/all_gather | solution.py:45
  95.4 198.4 %copy-start.63 = (f32[1,1,1024]{2,1,0:T(1,128)}, f32[1,1,1024]{2,1,0:T(1,128)S(1)}, u32[]{:S(2)}) copy-start(f32[1,1,1024]{2,1,0:T(1,128)S(1)} %get-tuple-element.78) | copy-start | bytes 12292
  299.5 61.7 %all-gather.41.cloned.1.call-start = ((), (), s32[]{:S(2)}) async-start(), calls=%async_computation.33 | async-start | bytes 2621440 | tf_op jit(solution)/shard_map/all_gather | solution.py:274
  300.3 117.9 %all-gather.43.cloned.1.call-start = ((), (), s32[]{:S(2)}) async-start(), calls=%async_computation.34 | async-start | bytes 10485760 | tf_op jit(solution)/shard_map/all_gather | solution.py:275
  301.0 177.5 %all-gather.45.cloned.1.call-start = ((), (), s32[]{:S(2)}) async-start(), calls=%async_computation.35 | async-start | bytes 10485760 | tf_op jit(solution)/shard_map/all_gather | solution.py:276
  301.6 279.3 %reduce-scatter.29.cloned.1.call-start = ((), (), s32[]{:S(2)}) async-start(), calls=%async_computation.18 | async-start | bytes 5242880 | tf_op jit(solution)/shard_map/reduce_scatter | solution.py:173
  363.9 130.3 %copy-start.78 = (f32[256]{0:T(256)}, f32[256]{0:T(256)S(1)}, u32[]{:S(2)}) copy-start(f32[256]{0:T(256)S(1)} %broadcast_multiply_fusion) | copy-start | bytes 3076
  364.1 130.0 %copy-start.88 = (f32[256]{0:T(256)}, f32[256]{0:T(256)S(1)}, u32[]{:S(2)}) copy-start(f32[256]{0:T(256)S(1)} %fusion.165) | copy-start | bytes 3076
  364.2 134.0 %copy-start.52 = (f32[16,256]{1,0:T(8,128)}, f32[16,256]{1,0:T(8,128)S(1)}, u32[]{:S(2)}) copy-start(f32[16,256]{1,0:T(8,128)S(1)} %log_add_fusion.1) | copy-start | bytes 49156
  536.3 162.0 %reduce-scatter.31.cloned.1.call-start = ((), (), s32[]{:S(2)}) async-start(), calls=%async_computation.19 | async-start | bytes 5242880 | tf_op jit(solution)/shard_map/reduce_scatter | solution.py:173
  643.2 83.2 %reduce-scatter.39.cloned.1.call-start = ((), (), s32[]{:S(2)}) async-start(), calls=%async_computation.23 | async-start | bytes 2621440 | tf_op jit(solution)/shard_map/reduce_scatter | solution.py:306
  646.4 110.0 %reduce-scatter.37.cloned.1.call-start = ((), (), s32[]{:S(2)}) async-start(), calls=%async_computation.22 | async-start | bytes 2621440 | tf_op jit(solution)/shard_map/reduce_scatter | solution.py:306
  648.6 182.1 %reduce-scatter.47.cloned.1.call-start = ((), (), s32[]{:S(2)}) async-start(), calls=%async_computation.27 | async-start | bytes 10485760 | tf_op jit(solution)/shard_map/reduce_scatter | solution.py:312
  657.3 248.3 %reduce-scatter.43.cloned.1.call-start = ((), (), s32[]{:S(2)}) async-start(), calls=%async_computation.25 | async-start | bytes 10485760 | tf_op jit(solution)/shard_map/reduce_scatter | solution.py:309
  664.9 302.0 %reduce-scatter.35.cloned.1.call-start = ((), (), s32[]{:S(2)}) async-start(), calls=%async_computation.21 | async-start | bytes 7864320 | tf_op jit(solution)/shard_map/reduce_scatter | solution.py:303
  672.2 369.1 %reduce-scatter.45.cloned.1.call-start = ((), (), s32[]{:S(2)}) async-start(), calls=%async_computation.26 | async-start | bytes 10485760 | tf_op jit(solution)/shard_map/reduce_scatter | solution.py:312
  681.9 433.7 %reduce-scatter.41.cloned.1.call-start = ((), (), s32[]{:S(2)}) async-start(), calls=%async_computation.24 | async-start | bytes 10485760 | tf_op jit(solution)/shard_map/reduce_scatter | solution.py:309
  690.7 486.5 %reduce-scatter.33.cloned.1.call-start = ((), (), s32[]{:S(2)}) async-start(), calls=%async_computation.20 | async-start | bytes 7864320 | tf_op jit(solution)/shard_map/reduce_scatter | solution.py:303
  704.7 495.0 %reduce-scatter.55.cloned.1.call-start = ((), (), s32[]{:S(2)}) async-start(), calls=%async_computation.39 | async-start | bytes 327680
  710.3 512.1 %reduce-scatter.51.cloned.1.call-start = ((), (), s32[]{:S(2)}) async-start(), calls=%async_computation.37 | async-start | bytes 327680
  711.3 533.6 %reduce-scatter.59.cloned.1.call-start = ((), (), s32[]{:S(2)}) async-start(), calls=%async_computation.41 | async-start | bytes 327680
  713.7 553.7 %reduce-scatter.53.cloned.1.call-start = ((), (), s32[]{:S(2)}) async-start(), calls=%async_computation.38 | async-start | bytes 327680
  724.3 565.6 %reduce-scatter.49.cloned.1.call-start = ((), (), s32[]{:S(2)}) async-start(), calls=%async_computation.36 | async-start | bytes 327680
  725.3 587.2 %reduce-scatter.57.cloned.1.call-start = ((), (), s32[]{:S(2)}) async-start(), calls=%async_computation.40 | async-start | bytes 327680
  726.3 997.0 %all-reduce.7.cloned.1.call-start = ((), (), s32[]{:S(2)}) async-start(), calls=%async_computation.42 | async-start | bytes 25165824 | tf_op jit(solution)/shard_map/psum | solution.py:329
  (123 other events, 1894.4 us)
Sparse Core Ops, SparseCore 0:
  11.2 49.1 all-gather.30
  66.4 34.6 all-gather.26
  103.2 22.5 all-gather.32
  127.2 58.3 all-gather.34
  187.5 58.2 all-gather.36
  247.3 46.4 all-gather.38
  299.7 34.4 all-gather.28
  335.7 22.5 all-gather.40
  359.9 58.2 all-gather.42
  420.2 58.2 all-gather.44
  536.4 44.4 reduce-scatter.28
  643.3 44.5 reduce-scatter.30
  690.9 31.4 reduce-scatter.38
  725.0 31.4 reduce-scatter.36
  758.9 71.7 reduce-scatter.46
  833.8 71.6 reduce-scatter.42
  908.5 58.3 reduce-scatter.34
  969.5 71.7 reduce-scatter.44
  1043.9 71.7 reduce-scatter.40
  1118.8 58.3 reduce-scatter.32
  1179.6 20.0 reduce-scatter.54
  1202.3 20.0 reduce-scatter.50
  1224.8 19.9 reduce-scatter.58
  1247.3 20.0 reduce-scatter.52
  1269.9 19.9 reduce-scatter.48
  1292.4 20.0 reduce-scatter.56
  1317.9 405.2 all-reduce.6
where the time goes:
time: 1760 us; the launch traced here: 1750 us
  waiting for transfers between devices  1270 us (72%)
  matrix products  219 us (12%)
  blocking collectives  91 us (5%)
  local copies, waits for them, and re-layouts  78.3 us (4%)
  other arithmetic  63.4 us (4%)
    psum x1, waiting for transfers between devices, shards(): lax.psum(shares[0].astype(jnp.bfloat16), 'rep').astype(jnp.float32)  369 us
    reduce_scatter x2, waiting for transfers between devices, shards(): lax.psum_scatter(large[2].astype(jnp.bfloat16), 'grp', scatter_dimension=...  149 us
    reduce_scatter x2, waiting for transfers between devices, shards(): lax.psum_scatter(large[3].astype(jnp.bfloat16), 'grp', scatter_dimension=...  149 us
    reduce_scatter x2, waiting for transfers between devices, shards(): lax.psum_scatter(large[0].astype(jnp.bfloat16), 'grp', scatter_dimension=...  123 us
    unnamed x33, waiting for transfers between devices  109 us
    all_gather x2, waiting for transfers between devices, shards(): lax.all_gather(expand[index], 'grp', axis=0, tiled=True)  108 us
    all_gather x2, waiting for transfers between devices, shards(): lax.all_gather(contract[index], 'grp', axis=0, tiled=True)  105 us
    all_gather x2, waiting for transfers between devices, shards(): lax.all_gather(project_in[index], 'grp', axis=0, tiled=True)  66.5 us
  transfers between devices with their start and end apart: 27, of which 23 were waited for; matrix products, arithmetic and copies ran while one was open for 11% of the time, Pallas kernels for 0%

commit v1 on v0

v1 whole, which is shorter than its diff:
```python
import functools

import jax
import jax.numpy as jnp
from jax import lax
from jax.experimental import pallas as pl
from jax.experimental.pallas import tpu as pltpu
from jax.sharding import PartitionSpec as P

HEADS = 16
LANES = 128
F32 = jnp.float32
BF16 = jnp.bfloat16


def swap(value, flip):
    count = lax.axis_size("grp")
    return lax.ppermute(value, "grp", [(i, i ^ flip) for i in range(count)])


def spread(block):
    far = swap(block, 2)
    near = swap(block, 1)
    return jnp.concatenate([block, near, far, swap(far, 1)], 0)


def collect(parts):
    rows = parts.shape[0] // 4
    parts = parts.reshape(4, rows, parts.shape[1])
    got_far = swap(parts[3], 1)
    far = (parts[2].astype(F32) + got_far.astype(F32)).astype(BF16)
    got = swap(far, 2)
    near = swap(parts[1], 1)
    return parts[0].astype(F32) + near.astype(F32) + got.astype(F32)


def place_blocks(blocks, me):
    out = jnp.zeros((len(blocks),) + blocks[0].shape, blocks[0].dtype)
    for r, block in enumerate(blocks):
        out = lax.dynamic_update_index_in_dim(out, block, me ^ r, 0)
    return out


def exchange(value, me):
    got = []
    for r in range(4):
        piece = lax.dynamic_index_in_dim(value, me ^ r, 0, keepdims=False)
        got.append(swap(piece, r) if r else piece)
    return place_blocks(got, me)


def stages(count):
    sizes = {8: (2, 4), 32: (4, 2, 4)}.get(count, (count,))
    out, stride = [], 1
    for size in sizes:
        out.append((stride, size))
        stride *= size
    return out


def ring(value, stride, size):
    count = lax.axis_size("rep")
    pairs = []
    for i in range(count):
        here = (i // stride) % size
        pairs.append((i, i + ((here + 1) % size - here) * stride))
    return lax.ppermute(value, "rep", pairs)


def place_of(stride, size):
    return lax.rem(lax.div(lax.axis_index("rep"), stride), size)


def scatter_stage(value, axis, stride, size):
    here = place_of(stride, size)

    def chunk(index):
        return lax.dynamic_index_in_dim(value, index, axis, keepdims=False)

    moving = chunk(lax.rem(here + size - 1, size))
    for step in range(1, size):
        moving = ring(moving, stride, size)
        own = chunk(lax.rem(here + 2 * size - 1 - step, size))
        moving = (moving.astype(F32) + own.astype(F32)).astype(BF16)
    return moving


def gather_stage(value, axis, stride, size):
    here = place_of(stride, size)
    out = jnp.zeros(value.shape[:axis] + (size,) + value.shape[axis:], value.dtype)
    out = lax.dynamic_update_index_in_dim(out, value, here, axis)
    moving = value
    for step in range(1, size):
        moving = ring(moving, stride, size)
        out = lax.dynamic_update_index_in_dim(out, moving, lax.rem(here + size - step, size), axis)
    return out


def replica_sum(value, turn, slow_first):
    count = lax.axis_size("rep")
    parts = stages(count)
    if slow_first:
        parts = parts[::-1]
    lead, rows, columns = value.shape
    sizes = [size for _, size in parts]
    value = value.reshape([lead] + sizes + [rows // count, columns])
    for stride, size in parts:
        value = scatter_stage(value, 1, stride, size)
    value = turn(value)
    for stride, size in parts[::-1]:
        value = gather_stage(value, 1, stride, size)
    return value.reshape((value.shape[0], rows) + value.shape[-1:])


def total_small(value):
    for flip in (1, 2):
        value = value + swap(value, flip)
    count = lax.axis_size("rep")
    flip = 1
    while flip < count:
        value = value + lax.ppermute(value, "rep", [(i, i ^ flip) for i in range(count)])
        flip *= 2
    return value


def dot(a, b, contract):
    return lax.dot_general(a, b, ((contract[:1], contract[1:]), ((), ())), preferred_element_type=F32)


def attend_kernel(me_ref, mixed_ref, out_ref, *, width, head, rows, blocks):
    me = me_ref[0]
    scale = head**-0.5
    which = lax.broadcasted_iota(jnp.int32, (rows, LANES), 1) // head
    below = lax.broadcasted_iota(jnp.int32, (rows, rows), 1) <= lax.broadcasted_iota(
        jnp.int32, (rows, rows), 0
    )
    for pair in range(width // LANES):
        column = pair * LANES

        def block(index, part):
            start = pl.multiple_of((me ^ index) * rows, rows)
            return mixed_ref[pl.ds(start, rows), part * width + column : part * width + column + LANES]

        keys = [block(j, 1) for j in range(blocks)]
        values = [block(j, 2) for j in range(blocks)]
        for i in range(blocks):
            query = block(i, 0) * jnp.asarray(scale, BF16)
            result = jnp.zeros((rows, LANES), F32)
            for h in range(LANES // head):
                mine = jnp.where(which == h, query, jnp.zeros_like(query))
                scores = [dot(mine, keys[j], (1, 1)) for j in range(i + 1)]
                scores[i] = jnp.where(below, scores[i], -1e30)
                top = functools.reduce(
                    jnp.maximum, [jnp.max(s, 1, keepdims=True) for s in scores]
                )
                exps = [jnp.exp(s - top) for s in scores]
                total = sum(jnp.sum(e, 1, keepdims=True) for e in exps)
                acc = sum(dot(e.astype(BF16), values[j], (1, 0)) for j, e in enumerate(exps))
                result = jnp.where(which == h, acc / total, result)
            start = pl.multiple_of((me ^ i) * rows, rows)
            out_ref[pl.ds(start, rows), column : column + LANES] = result.astype(BF16)


def attend_back_kernel(me_ref, mixed_ref, grad_ref, out_ref, *, width, head, rows, blocks):
    me = me_ref[0]
    scale = head**-0.5
    which = lax.broadcasted_iota(jnp.int32, (rows, LANES), 1) // head
    above = lax.broadcasted_iota(jnp.int32, (rows, rows), 0) <= lax.broadcasted_iota(
        jnp.int32, (rows, rows), 1
    )
    for pair in range(width // LANES):
        column = pair * LANES

        def place(index):
            return pl.ds(pl.multiple_of((me ^ index) * rows, rows), rows)

        def block(index, part):
            return mixed_ref[place(index), part * width + column : part * width + column + LANES]

        keys = [block(j, 1) for j in range(blocks)]
        values = [block(j, 2) for j in range(blocks)]
        d_keys = [jnp.zeros((rows, LANES), F32) for _ in range(blocks)]
        d_values = [jnp.zeros((rows, LANES), F32) for _ in range(blocks)]
        for i in range(blocks):
            query = block(i, 0) * jnp.asarray(scale, BF16)
            grad = grad_ref[place(i), column : column + LANES]
            d_query = jnp.zeros((rows, LANES), F32)
            for h in range(LANES // head):
                mine = jnp.where(which == h, query, jnp.zeros_like(query))
                mine_grad = jnp.where(which == h, grad, jnp.zeros_like(grad))
                scores = [dot(keys[j], mine, (1, 1)) for j in range(i + 1)]
                scores[i] = jnp.where(above, scores[i], -1e30)
                top = functools.reduce(
                    jnp.maximum, [jnp.max(s, 0, keepdims=True) for s in scores]
                )
                exps = [jnp.exp(s - top) for s in scores]
                inverse = 1.0 / sum(jnp.sum(e, 0, keepdims=True) for e in exps)
                probs = [e * inverse for e in exps]
                d_probs = [dot(values[j], mine_grad, (1, 1)) for j in range(i + 1)]
                inner = sum(jnp.sum(p * g, 0, keepdims=True) for p, g in zip(probs, d_probs))
                found = jnp.zeros((rows, LANES), F32)
                for j in range(i + 1):
                    d_score = (probs[j] * (d_probs[j] - inner)).astype(BF16)
                    d_keys[j] = d_keys[j] + dot(d_score, mine, (1, 0))
                    d_values[j] = d_values[j] + dot(probs[j].astype(BF16), mine_grad, (1, 0))
                    found = found + dot(d_score, keys[j], (0, 0))
                d_query = jnp.where(which == h, found, d_query)
            out_ref[place(i), column : column + LANES] = (d_query * scale).astype(BF16)
        for j in range(blocks):
            out_ref[place(j), width + column : width + column + LANES] = d_keys[j].astype(BF16)
            out_ref[place(j), 2 * width + column : 2 * width + column + LANES] = d_values[j].astype(BF16)


def attention(me, mixed, head, blocks, grad=None):
    length, triple = mixed.shape
    width = triple // 3
    sizes = dict(width=width, head=head, rows=length // blocks, blocks=blocks)
    heads = width // head
    half = length * length // 2
    if grad is None:
        kernel, arrays, out_width, products = attend_kernel, (mixed,), width, 2
    else:
        kernel, arrays, out_width, products = attend_back_kernel, (mixed, grad), triple, 5
    return pl.pallas_call(
        functools.partial(kernel, **sizes),
        out_shape=jax.ShapeDtypeStruct((length, out_width), BF16),
        in_specs=[pl.BlockSpec(memory_space=pltpu.SMEM)]
        + [pl.BlockSpec(memory_space=pltpu.VMEM)] * len(arrays),
        out_specs=pl.BlockSpec(memory_space=pltpu.VMEM),
        compiler_params=pltpu.CompilerParams(vmem_limit_bytes=40 * 2**20),
        cost_estimate=pl.CostEstimate(
            flops=products * 2 * half * heads * LANES * 2,
            bytes_accessed=length * triple * 4,
            transcendentals=half * heads,
        ),
    )(jnp.reshape(me, (1,)).astype(jnp.int32), *arrays)


def normed(values):
    average = jnp.mean(values, -1, keepdims=True)
    centered = values - average
    spread_of = jnp.mean(centered * centered, -1, keepdims=True)
    rate = lax.rsqrt(spread_of + 1e-05)
    return centered * rate, rate


def norm_back(incoming, values, gain):
    hat, rate = normed(values)
    scaled = incoming * gain
    first = jnp.mean(scaled, -1, keepdims=True)
    second = jnp.mean(scaled * hat, -1, keepdims=True)
    d_gain = jnp.sum(incoming * hat, 0)
    d_shift = jnp.sum(incoming, 0)
    return rate * (scaled - first - hat * second), d_gain, d_shift


def gelu_tanh(values):
    return jax.nn.gelu(values, approximate=True)


def shards(
    inputs,
    project_in,
    project_out,
    expand,
    contract,
    norm_gain,
    norm_shift,
    branch_bias,
    expand_bias,
    cotangent,
):
    layers = project_in.shape[0]
    rows, width = inputs.shape[1:]
    groups = lax.axis_size("grp")
    replicas = lax.axis_size("rep")
    head = width // HEADS
    part = width // groups
    hidden_part = expand.shape[2] // groups
    me = lax.axis_index("grp")
    replica = lax.axis_index("rep")

    def columns_by_device(weight, pieces):
        count = weight.shape[0]
        cut = weight.reshape(count, pieces, groups, -1)
        return cut.transpose(2, 0, 1, 3).reshape(groups, count, -1)

    in_columns = [None] * layers
    up_columns = [None] * layers
    in_columns[0] = exchange(columns_by_device(project_in[0], 3), me).reshape(width, 3 * part)
    slice_rows = part // replicas

    def slice_of(weight):
        return lax.dynamic_slice_in_dim(weight, replica * slice_rows, slice_rows, 0)

    wanted = []
    for index in range(layers):
        if index:
            wanted.append(("in", index, columns_by_device(slice_of(project_in[index]), 3)))
        wanted.append(("up", index, columns_by_device(slice_of(expand[index]), 1)))
    packed = exchange(jnp.concatenate([item[2] for item in wanted], -1), me)
    start = 0
    for kind, index, item in wanted:
        size = item.shape[-1]
        piece = packed[:, :, start : start + size]
        start += size
        whole = lax.all_gather(piece, "rep", axis=1, tiled=True).reshape(width, size)
        (in_columns if kind == "in" else up_columns)[index] = whole

    small = jnp.concatenate([norm_gain, norm_shift, branch_bias[:, 2:]], 1)
    small = lax.all_gather(small, "grp", axis=2, tiled=True).astype(F32)
    gains, shifts, out_biases = small[:, 0:2], small[:, 2:4], small[:, 4:6]
    mix_bias = jnp.concatenate(
        [branch_bias[:, 0], jnp.zeros_like(branch_bias[:, 0]), branch_bias[:, 1]], -1
    ).astype(F32)
    up_bias = expand_bias.astype(F32)

    state = inputs[0]
    saved = []
    for index in range(layers):
        hat, _ = normed(state)
        first = spread((hat * gains[index, 0] + shifts[index, 0]).astype(BF16))
        mixed = (dot(first, in_columns[index], (1, 0)) + mix_bias[index]).astype(BF16)
        attended = attention(me, mixed, head, groups)
        branch = dot(attended, project_out[index], (1, 0)).astype(BF16)
        middle = state + collect(branch) + out_biases[index, 0]
        hat, _ = normed(middle)
        second = spread((hat * gains[index, 1] + shifts[index, 1]).astype(BF16))
        raised = dot(second, up_columns[index], (1, 0)) + up_bias[index]
        active = gelu_tanh(raised).astype(BF16)
        down = dot(active, contract[index], (1, 0)).astype(BF16)
        saved.append((state, first, mixed, attended, middle, second, raised.astype(BF16), active))
        state = middle + collect(down) + out_biases[index, 1]

    grad = cotangent[0]
    grads = [None] * layers
    smalls = [None] * layers

    def keep(value):
        return value

    def turn_columns(pieces):
        def turn(value):
            got = exchange(value, me)
            count = got.shape[1]
            got = got.reshape(groups, count, pieces, -1).transpose(1, 2, 0, 3)
            return got.reshape(1, count, -1)

        return turn

    for index in reversed(range(layers)):
        before, first, mixed, attended, middle, second, raised, active = saved[index]
        d_down_own = grad.astype(BF16)
        d_down = spread(d_down_own)
        d_active = dot(d_down, contract[index], (1, 1))
        pull = jax.vjp(gelu_tanh, raised.astype(F32))[1]
        d_raised = pull(d_active)[0].astype(BF16)
        d_second = collect(dot(d_raised, up_columns[index], (1, 1)).astype(BF16))
        g_contract = dot(active, d_down, (0, 0)).astype(BF16)
        g_contract = replica_sum(g_contract[None], keep, False)[0]
        g_expand = dot(second, d_raised, (0, 0)).astype(BF16)
        g_expand = replica_sum(g_expand.reshape(groups, part, hidden_part), turn_columns(1), False)[0]
        d_up_bias = jnp.sum(d_raised.astype(F32), 0)
        d_middle, d_gain_two, d_shift_two = norm_back(d_second, middle, gains[index, 1])
        d_middle = grad + d_middle
        d_branch_own = d_middle.astype(BF16)
        d_branch = spread(d_branch_own)
        d_attended = dot(d_branch, project_out[index], (1, 1)).astype(BF16)
        d_mixed = attention(me, mixed, head, groups, d_attended)
        d_first = collect(dot(d_mixed, in_columns[index], (1, 1)).astype(BF16))
        g_out = dot(attended, d_branch, (0, 0)).astype(BF16)
        g_out = replica_sum(g_out[None], keep, True)[0]
        g_in = dot(first, d_mixed, (0, 0)).astype(BF16)
        g_in = replica_sum(g_in.reshape(groups, part, 3 * part), turn_columns(3), False)[0]
        d_mix_bias = jnp.sum(d_mixed.astype(F32), 0)
        d_first, d_gain_one, d_shift_one = norm_back(d_first, before, gains[index, 0])
        own_rows = [
            d_gain_one,
            d_gain_two,
            d_shift_one,
            d_shift_two,
            jnp.sum(d_branch_own.astype(F32), 0),
            jnp.sum(d_down_own.astype(F32), 0),
        ]
        own_part = jnp.concatenate([d_mix_bias[:part], d_mix_bias[2 * part :], d_up_bias])
        grads[index] = (g_in, g_out, g_expand, g_contract)
        smalls[index] = (jnp.stack(own_rows), own_part)
        grad = d_middle + d_first

    whole = jnp.stack([item[0] for item in smalls])
    owned = jnp.stack([item[1] for item in smalls])
    owned_all = jnp.zeros((groups,) + owned.shape, F32)
    owned_all = lax.dynamic_update_index_in_dim(owned_all, owned, me, 0)
    summed = total_small(jnp.concatenate([whole.reshape(-1), owned_all.reshape(-1)]))
    whole = summed[: whole.size].reshape(whole.shape)
    whole = lax.dynamic_slice_in_dim(whole, me * part, part, 2)
    owned = lax.dynamic_index_in_dim(
        summed[-owned_all.size :].reshape(owned_all.shape), me, 0, keepdims=False
    )
    merged = [
        jnp.stack([grads[index][member] for index in range(layers)]).astype(F32)
        for member in range(4)
    ]
    bias_grad = jnp.concatenate(
        [owned[:, None, :part], owned[:, None, part : 2 * part], whole[:, 4:6]], 1
    )
    return (
        state[None],
        grad[None],
        merged[0],
        merged[1],
        merged[2],
        merged[3],
        whole[:, 0:2],
        whole[:, 2:4],
        bias_grad,
        owned[:, 2 * part :],
    )


def solution(mesh):
    placed = (
        P("rep", "grp", None),
        P(None, "grp", None),
        P(None, "grp", None),
        P(None, "grp", None),
        P(None, "grp", None),
        P(None, None, "grp"),
        P(None, None, "grp"),
        P(None, None, "grp"),
        P(None, "grp"),
        P("rep", "grp", None),
    )
    return jax.shard_map(
        shards,
        mesh=mesh,
        in_specs=placed,
        out_specs=(
            P("rep", "grp", None),
            P("rep", "grp", None),
            P(None, "grp", None),
            P(None, "grp", None),
            P(None, "grp", None),
            P(None, "grp", None),
            P(None, None, "grp"),
            P(None, None, "grp"),
            P(None, None, "grp"),
            P(None, "grp"),
        ),
        check_vma=False,
    )
```

time: 1760 us -> 827 us (0.47)
  waiting for transfers between devices: 1270 us -> 428 us
  matrix products: 219 us -> 78.6 us
  blocking collectives: 91 us -> 6.2 us
  starting transfers between devices: 1.69 us -> 80 us
  Pallas kernels: 0 us -> 35.9 us
  local copies, waits for them, and re-layouts: 78.3 us -> 109 us
    reduce_scatter x10 -> x0, waiting for transfers between devices: 487 us -> none  [the longest x2 149 us: shards(): lax.psum_scatter(large[2].astype(jnp.bfloat16), 'grp', scatter_dimension=...]
    ppermute x0 -> x135, waiting for transfers between devices: none -> 411 us  [the longest x64 278 us: ring(): return lax.ppermute(value, 'rep', pairs)]
    psum x1 -> x0, waiting for transfers between devices: 369 us -> none  [shards(): lax.psum(shares[0].astype(jnp.bfloat16), 'rep').astype(jnp.float32)]
    all_gather x10 -> x3, waiting for transfers between devices: 309 us -> 17 us  [shards(): lax.all_gather(piece, 'rep', axis=1, tiled=True).reshape(width, size)]
    dot_general x36 -> x24, matrix products: 219 us -> 78.6 us  [dot(): lax.dot_general(a, b, ((contract[:1], contract[1:]), ((), ())), preferred...]
    unnamed x33 -> x3, waiting for transfers between devices: 109 us -> 0.05 us
    ppermute x0 -> x135, starting transfers between devices: none -> 79.7 us  [the longest x68 40.1 us: swap(): return lax.ppermute(value, 'grp', [(i, i ^ flip) for i in range(count)])]
    dynamic_update_slice x0 -> x66, local copies, waits for them, and re-layouts: none -> 42.5 us  [the longest x32 19.3 us: gather_stage(): lax.dynamic_update_index_in_dim(out, moving, lax.rem(here + size - step,...]
  transfers between devices with their start and end apart: 27 -> 138, of which waited for: 23 -> 67; matrix products, arithmetic and copies ran while one was open for 11% -> 28% of each run, Pallas kernels for 0% -> 4%
where the time goes in v1:
time: 827 us; the launch traced here: 820 us
  waiting for transfers between devices  428 us (52%)
  local copies, waits for them, and re-layouts  109 us (13%)
  starting transfers between devices  80 us (10%)
  matrix products  78.6 us (10%)
  other arithmetic  65.1 us (8%)
  Pallas kernels  35.9 us (4%)
  between operations  17 us (2%)
    ppermute x64, waiting for transfers between devices, ring(): return lax.ppermute(value, 'rep', pairs)  278 us
    ppermute x68, waiting for transfers between devices, swap(): return lax.ppermute(value, 'grp', [(i, i ^ flip) for i in range(count)])  122 us
    dot_general x24, matrix products, dot(): lax.dot_general(a, b, ((contract[:1], contract[1:]), ((), ())), preferred...  78.6 us
    ppermute x68, starting transfers between devices, swap(): return lax.ppermute(value, 'grp', [(i, i ^ flip) for i in range(count)])  40.1 us
    ppermute x64, starting transfers between devices, ring(): return lax.ppermute(value, 'rep', pairs)  38.3 us
    pallas_call x4, Pallas kernels, attention(): pl.pallas_call(functools.partial(kernel, **sizes), out_shape=jax.ShapeDty...  35.9 us
    dynamic_update_slice x32, local copies, waits for them, and re-layouts, gather_stage(): lax.dynamic_update_index_in_dim(out, moving, lax.rem(here + size - step,...  19.3 us
    all_gather x3, waiting for transfers between devices, shards(): lax.all_gather(piece, 'rep', axis=1, tiled=True).reshape(width, size)  17 us
  transfers between devices with their start and end apart: 138, of which 67 were waited for; matrix products, arithmetic and copies ran while one was open for 28% of the time, Pallas kernels for 4%

profile of v1, /device:TPU:0, one launch (start us, length us, event | category | flops | bytes accessed | tf_op | source)
XLA Modules:
  0.0 819.7 jit_solution(13172264729584835810)
XLA Ops:
  87.6 12.2 %collective-permute-done.8 = bf16[256,1024]{1,0:T(8,128)(2,1)S(1)} collective-permute-done((bf16[256,1024]{1,0:T(8,128)(2,1)S(1)}, bf16[256,1024]{1,0:T(8,128)(2,1)S(1)}, u32[]{:S(2)}, u32[]{:S(2)}) %collective-permute-start.8) | collective-permute-done | bytes 524320 | tf_op jit(solution)/shard_map/ppermute | solution.py:18
  102.6 11.8 %collective-permute-done.10 = bf16[256,1024]{1,0:T(8,128)(2,1)S(1)} collective-permute-done((bf16[256,1024]{1,0:T(8,128)(2,1)S(1)}, bf16[256,1024]{1,0:T(8,128)(2,1)S(1)}, u32[]{:S(2)}, u32[]{:S(2)}) %collective-permute-start.10) | collective-permute-done | bytes 524320 | tf_op jit(solution)/shard_map/ppermute | solution.py:18
  129.4 11.8 %collective-permute-done.17 = bf16[256,1024]{1,0:T(8,128)(2,1)S(1)} collective-permute-done((bf16[256,1024]{1,0:T(8,128)(2,1)S(1)}, bf16[256,1024]{1,0:T(8,128)(2,1)S(1)}, u32[]{:S(2)}, u32[]{:S(2)}) %collective-permute-start.17) | collective-permute-done | bytes 524320 | tf_op jit(solution)/shard_map/ppermute | solution.py:18
  145.3 11.7 %collective-permute-done.19 = bf16[256,1024]{1,0:T(8,128)(2,1)S(1)} collective-permute-done((bf16[256,1024]{1,0:T(8,128)(2,1)S(1)}, bf16[256,1024]{1,0:T(8,128)(2,1)S(1)}, u32[]{:S(2)}, u32[]{:S(2)}) %collective-permute-start.19) | collective-permute-done | bytes 524320 | tf_op jit(solution)/shard_map/ppermute | solution.py:18
  157.0 17.0 %all-gather.6.cloned.1.call-done = bf16[4,256,768]{2,1,0:T(8,128)(2,1)} async-done(((bf16[4,32,768]{2,1,0:T(8,128)(2,1)}), bf16[4,256,768]{2,1,0:T(8,128)(2,1)}) %all-gather.6.cloned.1.call-update) | async-done | bytes 1572880 | tf_op jit(solution)/shard_map/all_gather | solution.py:307
  189.2 12.5 %collective-permute-done.23 = bf16[256,1024]{1,0:T(8,128)(2,1)S(1)} collective-permute-done((bf16[256,1024]{1,0:T(8,128)(2,1)S(1)}, bf16[256,1024]{1,0:T(8,128)(2,1)S(1)}, u32[]{:S(2)}, u32[]{:S(2)}) %collective-permute-start.23) | collective-permute-done | bytes 524320 | tf_op jit(solution)/shard_map/ppermute | solution.py:18
  206.9 11.7 %collective-permute-done.25 = bf16[256,1024]{1,0:T(8,128)(2,1)} collective-permute-done((bf16[256,1024]{1,0:T(8,128)(2,1)}, bf16[256,1024]{1,0:T(8,128)(2,1)}, u32[]{:S(2)}, u32[]{:S(2)}) %collective-permute-start.25) | collective-permute-done | bytes 524320 | tf_op jit(solution)/shard_map/ppermute | solution.py:18
  219.1 9.0 %collective-permute-done.31 = bf16[256,1024]{1,0:T(8,128)(2,1)} collective-permute-done((bf16[256,1024]{1,0:T(8,128)(2,1)}, bf16[256,1024]{1,0:T(8,128)(2,1)}, u32[]{:S(2)}, u32[]{:S(2)}) %collective-permute-start.31) | collective-permute-done | bytes 524320 | tf_op jit(solution)/shard_map/ppermute | solution.py:18
  238.8 7.2 convert_reduce_fusion
  269.8 13.1 %collective-permute-done.122 = bf16[1,4,128,1024]{3,2,1,0:T(8,128)(2,1)} collective-permute-done((bf16[1,4,128,1024]{3,2,1,0:T(8,128)(2,1)}, bf16[1,4,128,1024]{3,2,1,0:T(8,128)(2,1)}, u32[]{:S(2)}, u32[]{:S(2)}) %collective-permute-start.122) | collective-permute-done | bytes 1048608 | tf_op jit(solution)/shard_map/ppermute | solution.py:67
  286.1 18.9 %collective-permute-done.103 = bf16[4,4,32,1024]{3,2,0,1:T(8,128)(2,1)} collective-permute-done((bf16[4,4,32,1024]{3,2,0,1:T(8,128)(2,1)}, bf16[4,4,32,1024]{3,2,0,1:T(8,128)(2,1)}, u32[]{:S(2)}, u32[]{:S(2)}) %collective-permute-start.103) | collective-permute-done | bytes 1048608 | tf_op jit(solution)/shard_map/ppermute | solution.py:67
  310.9 9.7 %collective-permute-done.104 = bf16[4,32,1024]{2,1,0:T(8,128)(2,1)S(1)} collective-permute-done((bf16[4,32,1024]{2,1,0:T(8,128)(2,1)S(1)}, bf16[4,32,1024]{2,1,0:T(8,128)(2,1)S(1)}, u32[]{:S(2)}, u32[]{:S(2)}) %collective-permute-start.104) | collective-permute-done | bytes 262176 | tf_op jit(solution)/shard_map/ppermute | solution.py:67
  372.5 12.0 %shard_map.179 = bf16[1024,768]{1,0:T(8,128)(2,1)S(1)} custom-call(s32[1]{0:T(128)} %bitcast.1.me_ref, bf16[1024,768]{1,0:T(8,128)(2,1)S(1)} %add_convert_fusion.2.mixed_ref, bf16[1024,256]{1,0:T(8,128)(2,1)S(1)} %convolution_convert_fusion.15.grad_ref), custom_call_target="tpu_custom_call" | custom-call | flops 5368709120 | bytes 3145728 | tf_op jit(solution)/shard_map/pallas_call | solution.py:224
  405.3 9.8 %collective-permute-done.86 = bf16[1,2,32,1024]{3,2,1,0:T(8,128)(2,1)S(1)} collective-permute-done((bf16[1,2,32,1024]{3,2,1,0:T(8,128)(2,1)S(1)}, bf16[1,2,32,1024]{3,2,1,0:T(8,128)(2,1)S(1)}, u32[]{:S(2)}, u32[]{:S(2)}) %collective-permute-start.86) | collective-permute-done | bytes 131104 | tf_op jit(solution)/shard_map/ppermute | solution.py:67
  439.0 6.7 collective-permute-done.90
  446.9 6.5 collective-permute-done.91
  453.4 7.9 collective-permute-done.66
  469.0 7.4 collective-permute-done.68
  482.6 11.9 %collective-permute-done.70 = bf16[32,768]{1,0:T(8,128)(2,1)S(1)} collective-permute-done((bf16[32,768]{1,0:T(8,128)(2,1)S(1)}, bf16[32,768]{1,0:T(8,128)(2,1)S(1)}, u32[]{:S(2)}, u32[]{:S(2)}) %collective-permute-start.70) | collective-permute-done | bytes 49184 | tf_op jit(solution)/shard_map/ppermute | solution.py:18
  503.1 7.1 collective-permute-done.72
  518.3 7.4 collective-permute-done.74
  526.7 8.0 convert_reduce_fusion.1
  551.5 16.9 %collective-permute-done.92 = bf16[4,4,32,1024]{3,2,0,1:T(8,128)(2,1)S(1)} collective-permute-done((bf16[4,4,32,1024]{3,2,0,1:T(8,128)(2,1)S(1)}, bf16[4,4,32,1024]{3,2,0,1:T(8,128)(2,1)S(1)}, u32[]{:S(2)}, u32[]{:S(2)}) %collective-permute-start.92) | collective-permute-done | bytes 1048608 | tf_op jit(solution)/shard_map/ppermute | solution.py:67
  570.1 19.1 %collective-permute-done.114 = bf16[1,4,128,1024]{3,2,1,0:T(8,128)(2,1)S(1)} collective-permute-done((bf16[1,4,128,1024]{3,2,1,0:T(8,128)(2,1)S(1)}, bf16[1,4,128,1024]{3,2,1,0:T(8,128)(2,1)S(1)}, u32[]{:S(2)}, u32[]{:S(2)}) %collective-permute-start.114) | collective-permute-done | bytes 1048608 | tf_op jit(solution)/shard_map/ppermute | solution.py:67
  592.9 7.9 collective-permute-done.115
  632.9 12.0 %shard_map.180 = bf16[1024,768]{1,0:T(8,128)(2,1)S(1)} custom-call(s32[1]{0:T(128)} %bitcast.1.me_ref, bf16[1024,768]{1,0:T(8,128)(2,1)S(1)} %copy-done.3, bf16[1024,256]{1,0:T(8,128)(2,1)S(1)} %convolution_convert_fusion.14.grad_ref), custom_call_target="tpu_custom_call" | custom-call | flops 5368709120 | bytes 3145728 | tf_op jit(solution)/shard_map/pallas_call | solution.py:224
  671.2 6.8 collective-permute-done.78
  703.7 7.6 collective-permute-done.82
  754.6 10.9 %collective-permute-done.134 = f32[24576]{0:T(1024)S(1)} collective-permute-done((f32[24576]{0:T(1024)S(1)}, f32[24576]{0:T(1024)S(1)}, u32[]{:S(2)}, u32[]{:S(2)}) %collective-permute-start.134) | collective-permute-done | bytes 98336 | tf_op jit(solution)/shard_map/ppermute | solution.py:121
  776.9 7.2 collective-permute-done.62
  784.1 7.8 collective-permute-done.63
  798.9 10.7 %collective-permute-done.64 = bf16[1,4,32,3072]{3,2,1,0:T(8,128)(2,1)S(1)} collective-permute-done((bf16[1,4,32,3072]{3,2,1,0:T(8,128)(2,1)S(1)}, bf16[1,4,32,3072]{3,2,1,0:T(8,128)(2,1)S(1)}, u32[]{:S(2)}, u32[]{:S(2)}) %collective-permute-start.64) | collective-permute-done | bytes 786464 | tf_op jit(solution)/shard_map/ppermute | solution.py:67
  (750 shorter events, 464.4 us)
Async XLA Ops:
  7.2 109.3 %all-gather.4.cloned.1.call-start = ((), (), s32[]{:S(2)}) async-start(), calls=%async_computation | async-start | bytes 2359296 | tf_op jit(solution)/shard_map/all_gather | solution.py:307
  18.9 44.5 %collective-permute-start.1 = (bf16[256,1024]{1,0:T(8,128)(2,1)}, bf16[256,1024]{1,0:T(8,128)(2,1)}, u32[]{:S(2)}, u32[]{:S(2)}) collective-permute-start(bf16[256,1024]{1,0:T(8,128)(2,1)} %add_convert_fusion.15), channel_id=1, source_target_pairs={{0,16},{8,24},{16,0},{24,8},{1,17},{9,25},{17,1},{25,9},{2,18},{10... | collective-permute-start | bytes 1572872 | tf_op jit(solution)/shard_map/ppermute | solution.py:18
  20.8 51.6 %collective-permute-start = (bf16[256,1024]{1,0:T(8,128)(2,1)}, bf16[256,1024]{1,0:T(8,128)(2,1)}, u32[]{:S(2)}, u32[]{:S(2)}) collective-permute-start(bf16[256,1024]{1,0:T(8,128)(2,1)} %add_convert_fusion.15), channel_id=1, source_target_pairs={{0,8},{8,0},{16,24},{24,16},{1,9},{9,1},{17,25},{25,17},{2,10},{10... | collective-permute-start | bytes 1572872 | tf_op jit(solution)/shard_map/ppermute | solution.py:18
  32.2 31.7 %collective-permute-start.3 = (bf16[256,768]{1,0:T(8,128)(2,1)}, bf16[256,768]{1,0:T(8,128)(2,1)}, u32[]{:S(2)}, u32[]{:S(2)}) collective-permute-start(bf16[256,768]{1,0:T(8,128)(2,1)} %bitcast.7), channel_id=1, source_target_pairs={{0,8},{8,0},{16,24},{24,16},{1,9},{9,1},{17,25},{25,17},{2,10},{10... | collective-permute-start | bytes 1179656 | tf_op jit(solution)/shard_map/ppermute | solution.py:18
  33.6 32.1 %collective-permute-start.4 = (bf16[256,768]{1,0:T(8,128)(2,1)}, bf16[256,768]{1,0:T(8,128)(2,1)}, u32[]{:S(2)}, u32[]{:S(2)}) collective-permute-start(bf16[256,768]{1,0:T(8,128)(2,1)} %bitcast.9), channel_id=1, source_target_pairs={{0,16},{8,24},{16,0},{24,8},{1,17},{9,25},{17,1},{25,9},{2,18},{10... | collective-permute-start | bytes 1179656 | tf_op jit(solution)/shard_map/ppermute | solution.py:18
  63.1 110.9 %all-gather.6.cloned.1.call-start = ((), (), s32[]{:S(2)}) async-start(), calls=%async_computation.1 | async-start | bytes 1769472 | tf_op jit(solution)/shard_map/all_gather | solution.py:307
  129.3 98.8 %all-gather.8.cloned.1.call-start = ((), (), s32[]{:S(2)}) async-start(), calls=%async_computation.2 | async-start | bytes 2359296 | tf_op jit(solution)/shard_map/all_gather | solution.py:307
  263.4 41.6 %collective-permute-start.103 = (bf16[4,4,32,1024]{3,2,0,1:T(8,128)(2,1)}, bf16[4,4,32,1024]{3,2,0,1:T(8,128)(2,1)}, u32[]{:S(2)}, u32[]{:S(2)}) collective-permute-start(bf16[4,4,32,1024]{3,2,0,1:T(8,128)(2,1)} %bitcast.462), channel_id=1, source_target_pairs={{0,1},{1,0},{2,3},{3,2},{4,5},{5,4},{6,7},{7,6},{8,9},{9,8},{10,11... | collective-permute-start | bytes 3145736 | tf_op jit(solution)/shard_map/ppermute | solution.py:67
  264.9 44.1 %collective-permute-start.33 = (bf16[256,1024]{1,0:T(8,128)(2,1)}, bf16[256,1024]{1,0:T(8,128)(2,1)S(1)}, u32[]{:S(2)}, u32[]{:S(2)}) collective-permute-start(bf16[256,1024]{1,0:T(8,128)(2,1)} %get-tuple-element.67), channel_id=1, source_target_pairs={{0,8},{8,0},{16,24},{24,16},{1,9},{9,1},{17,25},{25,17},{2,10},{10... | collective-permute-start | bytes 1572872 | tf_op jit(solution)/shard_map/ppermute | solution.py:18
  264.9 56.0 %collective-permute-start.27 = (bf16[256,1024]{1,0:T(8,128)(2,1)}, bf16[256,1024]{1,0:T(8,128)(2,1)S(1)}, u32[]{:S(2)}, u32[]{:S(2)}) collective-permute-start(bf16[256,1024]{1,0:T(8,128)(2,1)} %get-tuple-element.69), channel_id=1, source_target_pairs={{0,8},{8,0},{16,24},{24,16},{1,9},{9,1},{17,25},{25,17},{2,10},{10... | collective-permute-start | bytes 1572872 | tf_op jit(solution)/shard_map/ppermute | solution.py:18
  266.9 54.0 %collective-permute-start.29 = (bf16[256,1024]{1,0:T(8,128)(2,1)S(1)}, bf16[256,1024]{1,0:T(8,128)(2,1)S(1)}, u32[]{:S(2)}, u32[]{:S(2)}) collective-permute-start(bf16[256,1024]{1,0:T(8,128)(2,1)S(1)} %add_convert_fusion.8), channel_id=1, source_target_pairs={{0,16},{8,24},{16,0},{24,8},{1,17},{9,25},{17,1},{25,9},{2,18},{10... | collective-permute-start | bytes 1572872 | tf_op jit(solution)/shard_map/ppermute | solution.py:18
  331.5 38.7 %collective-permute-start.36 = (bf16[256,1024]{1,0:T(8,128)(2,1)}, bf16[256,1024]{1,0:T(8,128)(2,1)}, u32[]{:S(2)}, u32[]{:S(2)}) collective-permute-start(bf16[256,1024]{1,0:T(8,128)(2,1)} %get-tuple-element.37), channel_id=1, source_target_pairs={{0,8},{8,0},{16,24},{24,16},{1,9},{9,1},{17,25},{25,17},{2,10},{10... | collective-permute-start | bytes 1572872 | tf_op jit(solution)/shard_map/ppermute | solution.py:18
  338.7 31.6 %collective-permute-start.38 = (bf16[256,1024]{1,0:T(8,128)(2,1)}, bf16[256,1024]{1,0:T(8,128)(2,1)}, u32[]{:S(2)}, u32[]{:S(2)}) collective-permute-start(bf16[256,1024]{1,0:T(8,128)(2,1)} %collective-permute-done.37), channel_id=1, source_target_pairs={{0,8},{8,0},{16,24},{24,16},{1,9},{9,1},{17,25},{25,17},{2,10},{10... | collective-permute-start | bytes 1572872 | tf_op jit(solution)/shard_map/ppermute | solution.py:18
  362.2 35.4 %collective-permute-start.110 = (bf16[1,32,4096]{2,1,0:T(8,128)(2,1)}, bf16[1,32,4096]{2,1,0:T(8,128)(2,1)S(1)}, u32[]{:S(2)}, u32[]{:S(2)}) collective-permute-start(bf16[1,32,4096]{2,1,0:T(8,128)(2,1)} %reshape.599), channel_id=1, source_target_pairs={{0,2},{1,3},{2,4},{3,5},{4,6},{5,7},{6,0},{7,1},{8,10},{9,11},{10,... | collective-permute-start | bytes 786440 | tf_op jit(solution)/shard_map/ppermute | solution.py:67
  366.1 38.4 %collective-permute-start.127 = (bf16[1,128,1024]{2,1,0:T(8,128)(2,1)}, bf16[1,128,1024]{2,1,0:T(8,128)(2,1)S(1)}, u32[]{:S(2)}, u32[]{:S(2)}) collective-permute-start(bf16[1,128,1024]{2,1,0:T(8,128)(2,1)} %collective-permute-done.126), channel_id=1, source_target_pairs={{0,2},{1,3},{2,4},{3,5},{4,6},{5,7},{6,0},{7,1},{8,10},{9,11},{10,... | collective-permute-start | bytes 786440 | tf_op jit(solution)/shard_map/ppermute | solution.py:67
  386.7 45.5 %collective-permute-start.40 = (bf16[256,1024]{1,0:T(8,128)(2,1)S(1)}, bf16[256,1024]{1,0:T(8,128)(2,1)S(1)}, u32[]{:S(2)}, u32[]{:S(2)}) collective-permute-start(bf16[256,1024]{1,0:T(8,128)(2,1)S(1)} %get-tuple-element.66), channel_id=1, source_target_pairs={{0,8},{8,0},{16,24},{24,16},{1,9},{9,1},{17,25},{25,17},{2,10},{10... | collective-permute-start | bytes 1572872 | tf_op jit(solution)/shard_map/ppermute | solution.py:18
  386.8 74.7 %collective-permute-start.39 = (bf16[256,1024]{1,0:T(8,128)(2,1)S(1)}, bf16[256,1024]{1,0:T(8,128)(2,1)S(1)}, u32[]{:S(2)}, u32[]{:S(2)}) collective-permute-start(bf16[256,1024]{1,0:T(8,128)(2,1)S(1)} %get-tuple-element.65), channel_id=1, source_target_pairs={{0,8},{8,0},{16,24},{24,16},{1,9},{9,1},{17,25},{25,17},{2,10},{10... | collective-permute-start | bytes 1572872 | tf_op jit(solution)/shard_map/ppermute | solution.py:18
  397.0 49.5 %collective-permute-start.65 = (bf16[4,4,32,768]{3,2,0,1:T(8,128)(2,1)S(1)}, bf16[4,4,32,768]{3,2,0,1:T(8,128)(2,1)S(1)}, u32[]{:S(2)}, u32[]{:S(2)}) collective-permute-start(bf16[4,4,32,768]{3,2,0,1:T(8,128)(2,1)S(1)} %bitcast.497), channel_id=1, source_target_pairs={{0,1},{1,0},{2,3},{3,2},{4,5},{5,4},{6,7},{7,6},{8,9},{9,8},{10,11... | collective-permute-start | bytes 2359304 | tf_op jit(solution)/shard_map/ppermute | solution.py:67
  430.9 70.6 %collective-permute-start.129 = (bf16[1,4,128,1024]{3,2,1,0:T(8,128)(2,1)}, bf16[1,4,128,1024]{3,2,1,0:T(8,128)(2,1)}, u32[]{:S(2)}, u32[]{:S(2)}) collective-permute-start(bf16[1,4,128,1024]{3,2,1,0:T(8,128)(2,1)} %bitcast_dynamic-update-slice_fusion.15), channel_id=1, source_target_pairs={{0,1},{1,0},{2,3},{3,2},{4,5},{5,4},{6,7},{7,6},{8,9},{9,8},{10,11... | collective-permute-start | bytes 3145736 | tf_op jit(solution)/shard_map/ppermute | solution.py:67
  432.4 29.0 %collective-permute-start.41 = (bf16[256,1024]{1,0:T(8,128)(2,1)S(1)}, bf16[256,1024]{1,0:T(8,128)(2,1)S(1)}, u32[]{:S(2)}, u32[]{:S(2)}) collective-permute-start(bf16[256,1024]{1,0:T(8,128)(2,1)S(1)} %add_convert_fusion.6), channel_id=1, source_target_pairs={{0,16},{8,24},{16,0},{24,8},{1,17},{9,25},{17,1},{25,9},{2,18},{10... | collective-permute-start | bytes 1572872 | tf_op jit(solution)/shard_map/ppermute | solution.py:18
  445.7 64.5 %collective-permute-start.113 = (bf16[1,4,32,4096]{3,2,1,0:T(8,128)(2,1)}, bf16[1,4,32,4096]{3,2,1,0:T(8,128)(2,1)}, u32[]{:S(2)}, u32[]{:S(2)}) collective-permute-start(bf16[1,4,32,4096]{3,2,1,0:T(8,128)(2,1)} %bitcast_dynamic-update-slice_fusion.23), channel_id=1, source_target_pairs={{0,1},{1,0},{2,3},{3,2},{4,5},{5,4},{6,7},{7,6},{8,9},{9,8},{10,11... | collective-permute-start | bytes 3145736 | tf_op jit(solution)/shard_map/ppermute | solution.py:67
  480.0 46.7 %collective-permute-start.42 = (bf16[256,1024]{1,0:T(8,128)(2,1)}, bf16[256,1024]{1,0:T(8,128)(2,1)}, u32[]{:S(2)}, u32[]{:S(2)}) collective-permute-start(bf16[256,1024]{1,0:T(8,128)(2,1)} %get-tuple-element.29), channel_id=1, source_target_pairs={{0,8},{8,0},{16,24},{24,16},{1,9},{9,1},{17,25},{25,17},{2,10},{10... | collective-permute-start | bytes 1572872 | tf_op jit(solution)/shard_map/ppermute | solution.py:18
  525.8 80.7 %collective-permute-start.75 = (bf16[1,4,32,3072]{3,2,1,0:T(8,128)(2,1)S(1)}, bf16[1,4,32,3072]{3,2,1,0:T(8,128)(2,1)S(1)}, u32[]{:S(2)}, u32[]{:S(2)}) collective-permute-start(bf16[1,4,32,3072]{3,2,1,0:T(8,128)(2,1)S(1)} %bitcast_dynamic-update-slice_fusion.29), channel_id=1, source_target_pairs={{0,1},{1,0},{2,3},{3,2},{4,5},{5,4},{6,7},{7,6},{8,9},{9,8},{10,11... | collective-permute-start | bytes 2359304 | tf_op jit(solution)/shard_map/ppermute | solution.py:67
  537.3 31.7 %collective-permute-start.45 = (bf16[256,1024]{1,0:T(8,128)(2,1)S(1)}, bf16[256,1024]{1,0:T(8,128)(2,1)S(1)}, u32[]{:S(2)}, u32[]{:S(2)}) collective-permute-start(bf16[256,1024]{1,0:T(8,128)(2,1)S(1)} %get-tuple-element.63), channel_id=1, source_target_pairs={{0,8},{8,0},{16,24},{24,16},{1,9},{9,1},{17,25},{25,17},{2,10},{10... | collective-permute-start | bytes 1572872 | tf_op jit(solution)/shard_map/ppermute | solution.py:18
  548.6 40.6 %collective-permute-start.114 = (bf16[1,4,128,1024]{3,2,1,0:T(8,128)(2,1)S(1)}, bf16[1,4,128,1024]{3,2,1,0:T(8,128)(2,1)S(1)}, u32[]{:S(2)}, u32[]{:S(2)}) collective-permute-start(bf16[1,4,128,1024]{3,2,1,0:T(8,128)(2,1)S(1)} %dynamic-slice_bitcast_fusion.1), channel_id=1, source_target_pairs={{0,1},{1,0},{2,3},{3,2},{4,5},{5,4},{6,7},{7,6},{8,9},{9,8},{10,11... | collective-permute-start | bytes 3145736 | tf_op jit(solution)/shard_map/ppermute | solution.py:67
  623.8 31.7 %collective-permute-start.118 = (bf16[1,128,1024]{2,1,0:T(8,128)(2,1)S(1)}, bf16[1,128,1024]{2,1,0:T(8,128)(2,1)}, u32[]{:S(2)}, u32[]{:S(2)}) collective-permute-start(bf16[1,128,1024]{2,1,0:T(8,128)(2,1)S(1)} %get-tuple-element.40), channel_id=1, source_target_pairs={{0,2},{1,3},{2,4},{3,5},{4,6},{5,7},{6,0},{7,1},{8,10},{9,11},{10,... | collective-permute-start | bytes 786440 | tf_op jit(solution)/shard_map/ppermute | solution.py:67
  628.5 40.6 %collective-permute-start.99 = (bf16[1,32,4096]{2,1,0:T(8,128)(2,1)}, bf16[1,32,4096]{2,1,0:T(8,128)(2,1)}, u32[]{:S(2)}, u32[]{:S(2)}) collective-permute-start(bf16[1,32,4096]{2,1,0:T(8,128)(2,1)} %reshape.594), channel_id=1, source_target_pairs={{0,2},{1,3},{2,4},{3,5},{4,6},{5,7},{6,0},{7,1},{8,10},{9,11},{10,... | collective-permute-start | bytes 786440 | tf_op jit(solution)/shard_map/ppermute | solution.py:67
  648.1 47.6 %collective-permute-start.52 = (bf16[256,1024]{1,0:T(8,128)(2,1)}, bf16[256,1024]{1,0:T(8,128)(2,1)}, u32[]{:S(2)}, u32[]{:S(2)}) collective-permute-start(bf16[256,1024]{1,0:T(8,128)(2,1)} %get-tuple-element.62), channel_id=1, source_target_pairs={{0,8},{8,0},{16,24},{24,16},{1,9},{9,1},{17,25},{25,17},{2,10},{10... | collective-permute-start | bytes 1572872 | tf_op jit(solution)/shard_map/ppermute | solution.py:18
  648.7 78.8 %collective-permute-start.51 = (bf16[256,1024]{1,0:T(8,128)(2,1)}, bf16[256,1024]{1,0:T(8,128)(2,1)S(1)}, u32[]{:S(2)}, u32[]{:S(2)}) collective-permute-start(bf16[256,1024]{1,0:T(8,128)(2,1)} %get-tuple-element.61), channel_id=1, source_target_pairs={{0,8},{8,0},{16,24},{24,16},{1,9},{9,1},{17,25},{25,17},{2,10},{10... | collective-permute-start | bytes 1572872 | tf_op jit(solution)/shard_map/ppermute | solution.py:18
  655.5 56.9 %collective-permute-start.54 = (bf16[4,4,32,768]{3,2,0,1:T(8,128)(2,1)}, bf16[4,4,32,768]{3,2,0,1:T(8,128)(2,1)S(1)}, u32[]{:S(2)}, u32[]{:S(2)}) collective-permute-start(bf16[4,4,32,768]{3,2,0,1:T(8,128)(2,1)} %bitcast.465), channel_id=1, source_target_pairs={{0,1},{1,0},{2,3},{3,2},{4,5},{5,4},{6,7},{7,6},{8,9},{9,8},{10,11... | collective-permute-start | bytes 2359304 | tf_op jit(solution)/shard_map/ppermute | solution.py:67
  695.7 71.8 %collective-permute-start.121 = (bf16[1,4,128,1024]{3,2,1,0:T(8,128)(2,1)}, bf16[1,4,128,1024]{3,2,1,0:T(8,128)(2,1)}, u32[]{:S(2)}, u32[]{:S(2)}) collective-permute-start(bf16[1,4,128,1024]{3,2,1,0:T(8,128)(2,1)} %bitcast_dynamic-update-slice_fusion.19), channel_id=1, source_target_pairs={{0,1},{1,0},{2,3},{3,2},{4,5},{5,4},{6,7},{7,6},{8,9},{9,8},{10,11... | collective-permute-start | bytes 3145736 | tf_op jit(solution)/shard_map/ppermute | solution.py:67
  711.3 64.3 %collective-permute-start.102 = (bf16[1,4,32,4096]{3,2,1,0:T(8,128)(2,1)}, bf16[1,4,32,4096]{3,2,1,0:T(8,128)(2,1)}, u32[]{:S(2)}, u32[]{:S(2)}) collective-permute-start(bf16[1,4,32,4096]{3,2,1,0:T(8,128)(2,1)} %bitcast_dynamic-update-slice_fusion.26), channel_id=1, source_target_pairs={{0,1},{1,0},{2,3},{3,2},{4,5},{5,4},{6,7},{7,6},{8,9},{9,8},{10,11... | collective-permute-start | bytes 3145736 | tf_op jit(solution)/shard_map/ppermute | solution.py:67
  (201 other events, 2312.0 us)
Sparse Core Ops, SparseCore 0:
  63.3 49.7 all-gather.3
  129.4 44.5 all-gather.5
  176.8 48.0 all-gather.7

commit v2 on v1

v2 whole, which is shorter than its diff:
```python
import functools
import math

import jax
import jax.numpy as jnp
from jax import lax
from jax.experimental import pallas as pl
from jax.experimental.pallas import tpu as pltpu
from jax.sharding import PartitionSpec as P

HEADS = 16
LANES = 128
F32 = jnp.float32
BF16 = jnp.bfloat16


def swap(value, flip):
    count = lax.axis_size("grp")
    return lax.ppermute(value, "grp", [(i, i ^ flip) for i in range(count)])


def spread(block):
    far = swap(block, 2)
    near = swap(block, 1)
    return jnp.concatenate([block, near, far, swap(far, 1)], 0)


def collect(parts):
    rows = parts.shape[0] // 4
    parts = parts.reshape(4, rows, parts.shape[1])
    got_far = swap(parts[3], 1)
    far = (parts[2].astype(F32) + got_far.astype(F32)).astype(BF16)
    got = swap(far, 2)
    near = swap(parts[1], 1)
    return parts[0].astype(F32) + near.astype(F32) + got.astype(F32)


def exchange(value, me):
    got = [
        swap(lax.dynamic_index_in_dim(value, me ^ r, 0, keepdims=False), r)
        for r in range(1, lax.axis_size("grp"))
    ]
    got = yield got
    out = value
    for r, block in enumerate(got, 1):
        out = lax.dynamic_update_index_in_dim(out, block, me ^ r, 0)
    return out


def at_once(task):
    try:
        got = next(task)
        while True:
            got = task.send(got)
    except StopIteration as end:
        return end.value


def cross(value, bit):
    count = lax.axis_size("rep")
    return lax.ppermute(value, "rep", [(i, i ^ bit) for i in range(count)])


def tied(values, anchor):
    if anchor is None:
        return values
    return list(lax.optimization_barrier(tuple(values) + (anchor,))[:-1])


def replica_bits():
    count = lax.axis_size("rep")
    bits = [1]
    while 2 * bits[-1] < count:
        bits.append(2 * bits[-1])
    return bits


def replica_sum(value, turn, order):
    here = lax.axis_index("rep")
    chunks, rows, columns = value.shape
    for bit in order:
        mine = lax.rem(lax.div(here, bit), 2)
        value = value.reshape(2, -1, rows, columns)
        sent = lax.dynamic_index_in_dim(value, 1 - mine, 0, keepdims=False)
        (got,) = yield [cross(sent, bit)]
        own = lax.dynamic_index_in_dim(value, mine, 0, keepdims=False)
        value = (own.astype(F32) + got.astype(F32)).astype(BF16)
    value = value[0] if turn is None else (yield from turn(value[0]))
    value = value[None]
    for bit in order[::-1]:
        low = lax.rem(lax.div(here, bit), 2) == 0
        (got,) = yield [cross(value, bit)]
        value = jnp.concatenate([jnp.where(low, value, got), jnp.where(low, got, value)], 0)
    return value


class Rounds:
    def __init__(self):
        self.going = {}
        self.arriving = {}
        self.done = {}

    def add(self, name, task):
        self.going[name] = task
        self.arriving[name] = None
        self.step(name)

    def step(self, *names):
        for name in names:
            try:
                self.arriving[name] = self.going[name].send(self.arriving[name])
            except StopIteration as end:
                self.done[name] = end.value
                del self.going[name], self.arriving[name]

    def meet(self, values, *names):
        values, got = lax.optimization_barrier((values, [self.arriving[name] for name in names]))
        self.arriving.update(zip(names, got))
        self.step(*names)
        return values


def total_small(value):
    for flip in (1, 2):
        (got,) = yield [swap(value, flip)]
        value = value + got
    bit = 1
    while bit < lax.axis_size("rep"):
        (got,) = yield [cross(value, bit)]
        value = value + got
        bit *= 2
    return value


def dot(a, b, contract):
    return lax.dot_general(a, b, ((contract[:1], contract[1:]), ((), ())), preferred_element_type=F32)


def row_blocks(length, rows):
    return [slice(start, start + rows) for start in range(0, length, rows)]


def attend_kernel(
    me_ref, first_ref, into_ref, bias_ref, back_ref, mixed_ref, out_ref, part_ref, *, head, blocks
):
    me = me_ref[0]
    length, width = out_ref.shape
    rows = length // blocks
    scale = head**-0.5
    for block in row_blocks(length, rows):
        mixed_ref[block] = (dot(first_ref[block], into_ref[...], (1, 0)) + bias_ref[...]).astype(BF16)
    which = lax.broadcasted_iota(jnp.int32, (rows, LANES), 1) // head
    below = lax.broadcasted_iota(jnp.int32, (rows, rows), 1) <= lax.broadcasted_iota(
        jnp.int32, (rows, rows), 0
    )
    for pair in range(width // LANES):
        column = pair * LANES

        def block(index, part):
            start = pl.multiple_of((me ^ index) * rows, rows)
            return mixed_ref[pl.ds(start, rows), part * width + column : part * width + column + LANES]

        keys = [block(j, 1) for j in range(blocks)]
        values = [block(j, 2) for j in range(blocks)]
        for i in range(blocks):
            query = block(i, 0) * jnp.asarray(scale, BF16)
            result = jnp.zeros((rows, LANES), F32)
            for h in range(LANES // head):
                mine = jnp.where(which == h, query, jnp.zeros_like(query))
                scores = [dot(mine, keys[j], (1, 1)) for j in range(i + 1)]
                scores[i] = jnp.where(below, scores[i], -1e30)
                top = functools.reduce(
                    jnp.maximum, [jnp.max(s, 1, keepdims=True) for s in scores]
                )
                exps = [jnp.exp(s - top) for s in scores]
                total = sum(jnp.sum(e, 1, keepdims=True) for e in exps)
                acc = sum(dot(e.astype(BF16), values[j], (1, 0)) for j, e in enumerate(exps))
                result = jnp.where(which == h, acc / total, result)
            start = pl.multiple_of((me ^ i) * rows, rows)
            out_ref[pl.ds(start, rows), column : column + LANES] = result.astype(BF16)
    for block in row_blocks(length, rows):
        part_ref[block] = dot(out_ref[block], back_ref[...], (1, 0)).astype(BF16)


def attend_back_kernel(
    me_ref, mixed_ref, branch_ref, back_ref, into_ref, out_ref, part_ref, sums_ref, grad_ref, *, head, blocks
):
    me = me_ref[0]
    length, width = grad_ref.shape
    rows = length // blocks
    scale = head**-0.5
    for block in row_blocks(length, rows):
        grad_ref[block] = dot(branch_ref[block], back_ref[...], (1, 1)).astype(BF16)
    which = lax.broadcasted_iota(jnp.int32, (rows, LANES), 1) // head
    above = lax.broadcasted_iota(jnp.int32, (rows, rows), 0) <= lax.broadcasted_iota(
        jnp.int32, (rows, rows), 1
    )
    for pair in range(width // LANES):
        column = pair * LANES

        def place(index):
            return pl.ds(pl.multiple_of((me ^ index) * rows, rows), rows)

        def block(index, part):
            return mixed_ref[place(index), part * width + column : part * width + column + LANES]

        keys = [block(j, 1) for j in range(blocks)]
        values = [block(j, 2) for j in range(blocks)]
        d_keys = [jnp.zeros((rows, LANES), F32) for _ in range(blocks)]
        d_values = [jnp.zeros((rows, LANES), F32) for _ in range(blocks)]
        for i in range(blocks):
            query = block(i, 0) * jnp.asarray(scale, BF16)
            grad = grad_ref[place(i), column : column + LANES]
            d_query = jnp.zeros((rows, LANES), F32)
            for h in range(LANES // head):
                mine = jnp.where(which == h, query, jnp.zeros_like(query))
                mine_grad = jnp.where(which == h, grad, jnp.zeros_like(grad))
                scores = [dot(keys[j], mine, (1, 1)) for j in range(i + 1)]
                scores[i] = jnp.where(above, scores[i], -1e30)
                top = functools.reduce(
                    jnp.maximum, [jnp.max(s, 0, keepdims=True) for s in scores]
                )
                exps = [jnp.exp(s - top) for s in scores]
                inverse = 1.0 / sum(jnp.sum(e, 0, keepdims=True) for e in exps)
                probs = [e * inverse for e in exps]
                d_probs = [dot(values[j], mine_grad, (1, 1)) for j in range(i + 1)]
                inner = sum(jnp.sum(p * g, 0, keepdims=True) for p, g in zip(probs, d_probs))
                found = jnp.zeros((rows, LANES), F32)
                for j in range(i + 1):
                    d_score = (probs[j] * (d_probs[j] - inner)).astype(BF16)
                    d_keys[j] = d_keys[j] + dot(d_score, mine, (1, 0))
                    d_values[j] = d_values[j] + dot(probs[j].astype(BF16), mine_grad, (1, 0))
                    found = found + dot(d_score, keys[j], (0, 0))
                d_query = jnp.where(which == h, found, d_query)
            out_ref[place(i), column : column + LANES] = (d_query * scale).astype(BF16)
        for j in range(blocks):
            out_ref[place(j), width + column : width + column + LANES] = d_keys[j].astype(BF16)
            out_ref[place(j), 2 * width + column : 2 * width + column + LANES] = d_values[j].astype(BF16)
    total = jnp.zeros(sums_ref.shape, F32)
    for block in row_blocks(length, rows):
        mixed = out_ref[block]
        total = total + jnp.sum(mixed.astype(F32), 0, keepdims=True)
        part_ref[block] = dot(mixed, into_ref[...], (1, 1)).astype(BF16)
    sums_ref[...] = total


def feed_kernel(second_ref, up_ref, bias_ref, down_ref, active_ref, slope_ref, part_ref, *, blocks):
    length = second_ref.shape[0]
    root, cube = (2.0 / math.pi) ** 0.5, 0.044715
    for block in row_blocks(length, length // blocks):
        u = dot(second_ref[block], up_ref[...], (1, 0)) + bias_ref[...]
        t = jnp.tanh(root * (u + cube * u * u * u))
        active = (0.5 * u * (1.0 + t)).astype(BF16)
        active_ref[block] = active
        slope = 0.5 * (1.0 + t) + 0.5 * u * (1.0 - t * t) * root * (1.0 + 3.0 * cube * u * u)
        slope_ref[block] = slope.astype(BF16)
        part_ref[block] = dot(active, down_ref[...], (1, 0)).astype(BF16)


def feed_back_kernel(
    grad_ref, slope_ref, down_ref, up_ref, raised_ref, part_ref, sums_ref, *, blocks
):
    length = grad_ref.shape[0]
    total = jnp.zeros(sums_ref.shape, F32)
    for block in row_blocks(length, length // blocks):
        d_active = dot(grad_ref[block], down_ref[...], (1, 1))
        d_raised = (slope_ref[block].astype(F32) * d_active).astype(BF16)
        raised_ref[block] = d_raised
        total = total + jnp.sum(d_raised.astype(F32), 0, keepdims=True)
        part_ref[block] = dot(d_raised, up_ref[...], (1, 1)).astype(BF16)
    sums_ref[...] = total


def weights_kernel(*refs, blocks):
    out_ref = refs[-1]
    rows = out_ref.shape[0] // blocks
    start = 0
    for a_ref, b_ref in zip(refs[:-1:2], refs[1:-1:2]):
        size = b_ref.shape[1]
        for block in row_blocks(out_ref.shape[0], rows):
            out_ref[block, start : start + size] = dot(a_ref[:, block], b_ref[...], (0, 0)).astype(BF16)
        start += size


def kernel_call(kernel, arrays, outs, me=None, scratch=(), **sizes):
    scalars = [] if me is None else [jnp.reshape(me, (1,)).astype(jnp.int32)]
    return pl.pallas_call(
        functools.partial(kernel, **sizes),
        out_shape=[jax.ShapeDtypeStruct(shape, dtype) for shape, dtype in outs],
        in_specs=[pl.BlockSpec(memory_space=pltpu.SMEM)] * len(scalars)
        + [pl.BlockSpec(memory_space=pltpu.VMEM)] * len(arrays),
        out_specs=[pl.BlockSpec(memory_space=pltpu.VMEM)] * len(outs),
        scratch_shapes=list(scratch),
        compiler_params=pltpu.CompilerParams(vmem_limit_bytes=40 * 2**20),
        cost_estimate=pl.CostEstimate(flops=0, bytes_accessed=0, transcendentals=0),
    )(*scalars, *arrays)


def weight_products(*pairs, blocks):
    outs = [((pairs[0][0].shape[1], sum(b.shape[1] for _, b in pairs)), BF16)]
    return kernel_call(weights_kernel, [x for pair in pairs for x in pair], outs, blocks=blocks)[0]


def normed(values):
    average = jnp.mean(values, -1, keepdims=True)
    centered = values - average
    spread_of = jnp.mean(centered * centered, -1, keepdims=True)
    rate = lax.rsqrt(spread_of + 1e-05)
    return centered * rate, rate


def norm_back(incoming, values, gain):
    hat, rate = normed(values)
    scaled = incoming * gain
    first = jnp.mean(scaled, -1, keepdims=True)
    second = jnp.mean(scaled * hat, -1, keepdims=True)
    d_gain = jnp.sum(incoming * hat, 0)
    d_shift = jnp.sum(incoming, 0)
    return rate * (scaled - first - hat * second), d_gain, d_shift


def gelu_tanh(values):
    return jax.nn.gelu(values, approximate=True)


def shards(
    inputs,
    project_in,
    project_out,
    expand,
    contract,
    norm_gain,
    norm_shift,
    branch_bias,
    expand_bias,
    cotangent,
):
    layers = project_in.shape[0]
    rows, width = inputs.shape[1:]
    groups = lax.axis_size("grp")
    replicas = lax.axis_size("rep")
    head = width // HEADS
    part = width // groups
    hidden_part = expand.shape[2] // groups
    me = lax.axis_index("grp")
    replica = lax.axis_index("rep")

    def columns_by_device(weight, pieces):
        wide = weight.shape[1] // pieces
        size = wide // groups
        return jnp.stack(
            [
                jnp.concatenate(
                    [
                        weight[:, piece * wide + device * size : piece * wide + (device + 1) * size]
                        for piece in range(pieces)
                    ],
                    1,
                )
                for device in range(groups)
            ]
        )

    in_columns = [None] * layers
    up_columns = [None] * layers
    slice_rows = part // replicas

    def slices_by_device(weight, pieces):
        mine = lax.dynamic_slice_in_dim(weight, replica * slice_rows, slice_rows, 0)
        return columns_by_device(mine, pieces)

    def from_replicas(value):
        whole = lax.all_gather(value, "rep", axis=1, tiled=True)
        return whole.reshape(width, value.shape[-1])

    sent = slices_by_device(expand[0], 1)
    slice_up = at_once(exchange(sent, me))
    up_columns[0] = from_replicas(slice_up)
    sent = columns_by_device(tied([project_in[0]], sent)[0], 3)
    in_columns[0] = at_once(exchange(sent, me)).reshape(width, 3 * part)
    in_columns[0] = tied([in_columns[0]], slice_up)[0]
    slices = []
    for index in range(1, layers):
        pair = [slices_by_device(project_in[index], 3), slices_by_device(expand[index], 1)]
        both = at_once(exchange(tied([jnp.concatenate(pair, -1)], sent)[0], me))
        slices.append((both[..., : 3 * part], both[..., 3 * part :]))

    small = jnp.concatenate([norm_gain, norm_shift, branch_bias[:, 2:]], 1)
    small = lax.all_gather(small, "grp", axis=2, tiled=True).astype(F32)
    gains, shifts, out_biases = small[:, 0:2], small[:, 2:4], small[:, 4:6]
    mix_bias = jnp.concatenate(
        [branch_bias[:, 0], jnp.zeros_like(branch_bias[:, 0]), branch_bias[:, 1]], -1
    ).astype(F32)
    up_bias = expand_bias.astype(F32)

    state = inputs[0]
    saved = []
    for index in range(layers):
        hat, _ = normed(state)
        first = spread((hat * gains[index, 0] + shifts[index, 0]).astype(BF16))
        length = first.shape[0]
        mixed, attended, branch = kernel_call(
            attend_kernel,
            [first, in_columns[index], mix_bias[index : index + 1], project_out[index]],
            [((length, 3 * part), BF16), ((length, part), BF16), ((length, width), BF16)],
            me=me,
            head=head,
            blocks=groups,
        )
        if index < layers - 1:
            in_columns[index + 1] = from_replicas(tied([slices[index][0]], attended)[0])
        middle = state + collect(branch) + out_biases[index, 0]
        hat, _ = normed(middle)
        second = spread((hat * gains[index, 1] + shifts[index, 1]).astype(BF16))
        active, slope, down = kernel_call(
            feed_kernel,
            [second, up_columns[index], up_bias[index : index + 1], contract[index]],
            [((length, hidden_part), BF16)] * 2 + [((length, width), BF16)],
            blocks=groups,
        )
        if index < layers - 1:
            up_columns[index + 1] = from_replicas(tied([slices[index][1]], active)[0])
            state_after = middle + collect(down) + out_biases[index, 1]
        saved.append((state, first, mixed, attended, middle, second, slope, active, down))
        if index < layers - 1:
            state = state_after


    rounds = Rounds()

    def by_replica(value):
        cut = value.reshape(groups, replicas, slice_rows, value.shape[1])
        return cut.transpose(1, 0, 2, 3).reshape(replicas, groups * slice_rows, -1)

    def turn(value):
        got = yield from exchange(value.reshape(groups, -1, value.shape[-1]), me)
        return got.reshape(value.shape)

    def turn_both(value):
        turned = yield from turn(value[:, : 3 * part])
        return jnp.concatenate([turned, value[:, 3 * part :]], 1)

    bits = replica_bits()
    def feed_back(index, grad):
        second, slope, active = saved[index][5:8]
        d_down_own = grad.astype(BF16)
        d_down = spread(d_down_own)
        d_raised, partial, d_up_bias = kernel_call(
            feed_back_kernel,
            [d_down, slope, contract[index], up_columns[index]],
            [((length, hidden_part), BF16), ((length, width), BF16), ((1, hidden_part), F32)],
            blocks=groups,
        )
        early = tied([active, second], partial)
        g_contract = weight_products((early[0], d_down), blocks=groups)
        g_expand = weight_products((early[1], d_raised), blocks=groups)
        return g_contract, g_expand, (grad, d_down_own, partial, d_up_bias, g_expand)

    def norm_two_back(index, kept):
        grad, d_down_own, partial, d_up_bias, made = kept
        middle = saved[index][4]
        d_second = tied([collect(partial)], made)[0]
        d_middle, d_gain, d_shift = norm_back(d_second, middle, gains[index, 1])
        d_middle = grad + d_middle
        d_branch_own = d_middle.astype(BF16)
        sums = [jnp.sum(value.astype(F32), 0) for value in (d_branch_own, d_down_own)]
        return d_middle, spread(d_branch_own), [d_gain, d_shift] + sums, d_up_bias

    def attend_back(index, kept):
        d_middle, d_branch, (d_gain_two, d_shift_two, *sums), d_up_bias = kept
        before, first, mixed, attended, middle = saved[index][:5]
        state = None
        d_mixed, partial, d_mix_bias = kernel_call(
            attend_back_kernel,
            [mixed, d_branch, project_out[index], in_columns[index]],
            [((length, 3 * part), BF16), ((length, width), BF16), ((1, 3 * part), F32)],
            me=me,
            scratch=[pltpu.VMEM((length, part), BF16)],
            head=head,
            blocks=groups,
        )
        if index == layers - 1:
            down = tied([saved[index][8]], d_branch)[0]
            state = middle + collect(down) + out_biases[index, 1]
            partial = tied([partial], state)[0]
        early = tied([first, attended], partial)
        g_both = weight_products((early[0], d_mixed), (d_branch, early[1]), blocks=groups)
        d_first = tied([collect(partial)], g_both)[0]
        d_first, d_gain_one, d_shift_one = norm_back(d_first, before, gains[index, 0])
        own_rows = jnp.stack([d_gain_one, d_gain_two, d_shift_one, d_shift_two] + sums)
        own_part = jnp.concatenate([d_mix_bias[0, :part], d_mix_bias[0, 2 * part :], d_up_bias[0]])
        return g_both, (own_rows, own_part), d_middle + d_first, state

    def segment(run):
        shapes = jax.eval_shape(run)
        return lax.cond(
            replica < 4 * replicas,
            run,
            lambda: jax.tree.map(lambda leaf: jnp.zeros(leaf.shape, leaf.dtype), shapes),
        )

    def start_both(index, g_both):
        rounds.add("both %d" % index, replica_sum(by_replica(g_both), turn_both, bits))

    last = layers - 1
    small = [None] * layers
    g_contract, g_expand, kept = feed_back(last, cotangent[0])
    beside = lax.psum((g_contract, g_expand), "rep")

    def first_segment():
        g_both, small, grad, state = attend_back(last, norm_two_back(last, kept))
        return (g_both, small, state) + feed_back(0, grad)

    g_late, small[last], state, g_contract, g_expand, kept = segment(first_segment)
    rounds.add("contract 0", replica_sum(g_contract.reshape(replicas, -1, width), None, bits))
    kept = segment(lambda: norm_two_back(0, kept))
    kept, beside = lax.optimization_barrier((kept, beside))
    kept = rounds.meet(kept, "contract 0")
    rounds.add("expand 0", replica_sum(by_replica(g_expand), turn, bits))
    rounds.add("both 1", replica_sum(by_replica(g_late), turn_both, bits))
    g_both, small[0], grad, _ = segment(lambda: attend_back(0, kept))
    g_both = rounds.meet(g_both, "contract 0", "expand 0", "both 1")
    rounds.add("both 0", replica_sum(by_replica(g_both), turn_both, bits))
    rounds.done["contract 1"] = beside[0]
    rounds.add("expand 1", turn(beside[1]))

    whole = jnp.stack([item[0] for item in small])
    owned = jnp.stack([item[1] for item in small])
    owned_all = jnp.zeros((groups,) + owned.shape, F32)
    owned_all = lax.dynamic_update_index_in_dim(owned_all, owned, me, 0)
    rounds.step("contract 0", "expand 0", "both 1")
    both_small = tied([whole.reshape(-1), owned_all.reshape(-1)], rounds.arriving["expand 0"][0])
    rounds.add("small", total_small(jnp.concatenate(both_small)))
    while rounds.going:
        rounds.step(*rounds.going)

    grads = []
    for index in range(layers):
        g_contract, g_expand, g_both = [
            rounds.done["%s %d" % (name, index)] for name in ("contract", "expand", "both")
        ]

        def rows_from(value, source):
            if value.ndim == 2:
                return value[source * part : (source + 1) * part]
            return value.reshape(replicas, groups, slice_rows, -1)[:, source].reshape(part, -1)

        parts = [rows_from(g_both, source) for source in range(groups)]
        g_in = jnp.concatenate(
            [piece[:, kind * part : (kind + 1) * part] for kind in range(3) for piece in parts], 1
        )
        g_out = jnp.concatenate([piece[:, 3 * part :] for piece in parts], 0).T
        g_expand = jnp.concatenate([rows_from(g_expand, source) for source in range(groups)], 1)
        g_contract = g_contract.reshape(-1, width)
        each = (g_in, g_out, g_expand, g_contract)
        grads.append([lax.optimization_barrier(value) for value in each])

    summed = rounds.done["small"]
    whole = summed[: whole.size].reshape(whole.shape)
    whole = lax.dynamic_slice_in_dim(whole, me * part, part, 2)
    owned = lax.dynamic_index_in_dim(
        summed[-owned_all.size :].reshape(owned_all.shape), me, 0, keepdims=False
    )
    merged = [
        jnp.stack([grads[index][member] for index in range(layers)]).astype(F32)
        for member in range(4)
    ]
    bias_grad = jnp.concatenate(
        [owned[:, None, :part], owned[:, None, part : 2 * part], whole[:, 4:6]], 1
    )
    return (
        state[None],
        grad[None],
        merged[0],
        merged[1],
        merged[2],
        merged[3],
        whole[:, 0:2],
        whole[:, 2:4],
        bias_grad,
        owned[:, 2 * part :],
    )


def solution(mesh):
    placed = (
        P("rep", "grp", None),
        P(None, "grp", None),
        P(None, "grp", None),
        P(None, "grp", None),
        P(None, "grp", None),
        P(None, None, "grp"),
        P(None, None, "grp"),
        P(None, None, "grp"),
        P(None, "grp"),
        P("rep", "grp", None),
    )
    return jax.shard_map(
        shards,
        mesh=mesh,
        in_specs=placed,
        out_specs=(
            P("rep", "grp", None),
            P("rep", "grp", None),
            P(None, "grp", None),
            P(None, "grp", None),
            P(None, "grp", None),
            P(None, "grp", None),
            P(None, None, "grp"),
            P(None, None, "grp"),
            P(None, None, "grp"),
            P(None, "grp"),
        ),
        check_vma=False,
    )
```

time: 827 us -> 726 us (0.88)
  matrix products: 78.6 us -> 0 us
  Pallas kernels: 35.9 us -> 109 us
  waiting for transfers between devices: 428 us -> 359 us
  local copies, waits for them, and re-layouts: 109 us -> 70.3 us
  other arithmetic: 65.1 us -> 83.6 us
  starting transfers between devices: 80 us -> 70.7 us
    ppermute x67 -> x27, waiting for transfers between devices: 289 us -> 123 us  [cross(): return lax.ppermute(value, 'rep', [(i, i ^ bit) for i in range(count)])]
    ppermute x68 -> x71, waiting for transfers between devices: 122 us -> 204 us  [swap(): return lax.ppermute(value, 'grp', [(i, i ^ flip) for i in range(count)])]
    dot_general x24 -> x0, matrix products: 78.6 us -> none  [dot(): lax.dot_general(a, b, ((contract[:1], contract[1:]), ((), ())), preferred...]
    pallas_call x4 -> x14, Pallas kernels: 35.9 us -> 109 us  [kernel_call(): pl.pallas_call(functools.partial(kernel, **sizes), out_shape=[jax.ShapeDt...]
    dynamic_update_slice x66 -> x14, local copies, waits for them, and re-layouts: 42.5 us -> 3.11 us  [exchange(): out = lax.dynamic_update_index_in_dim(out, block, me ^ r, 0)]
    all_gather x3, waiting for transfers between devices: 17 us -> 32.5 us  [from_replicas(): whole = lax.all_gather(value, 'rep', axis=1, tiled=True)]
    concatenate x3 -> x25, other arithmetic: 0.33 us -> 14.2 us  [the longest x8 9.06 us: spread(): return jnp.concatenate([block, near, far, swap(far, 1)], 0)]
    squeeze x17 -> x32, local copies, waits for them, and re-layouts: 2.28 us -> 15.7 us  [the longest x12 7.24 us: replica_sum(): sent = lax.dynamic_index_in_dim(value, 1 - mine, 0, keepdims=False)]
  transfers between devices with their start and end apart: 138 -> 102, of which waited for: 67 -> 50; matrix products, arithmetic and copies ran while one was open for 28% -> 16% of each run, Pallas kernels for 4% -> 9%
where the time goes in v2:
time: 726 us; the launch traced here: 716 us
  waiting for transfers between devices  359 us (49%)
  Pallas kernels  109 us (15%)
  other arithmetic  83.6 us (12%)
  starting transfers between devices  70.7 us (10%)
  local copies, waits for them, and re-layouts  70.3 us (10%)
  between operations  16 us (2%)
    ppermute x71, waiting for transfers between devices, swap(): return lax.ppermute(value, 'grp', [(i, i ^ flip) for i in range(count)])  204 us
    ppermute x27, waiting for transfers between devices, cross(): return lax.ppermute(value, 'rep', [(i, i ^ bit) for i in range(count)])  123 us
    pallas_call x14, Pallas kernels, kernel_call(): pl.pallas_call(functools.partial(kernel, **sizes), out_shape=[jax.ShapeDt...  109 us
    ppermute x27, starting transfers between devices, cross(): return lax.ppermute(value, 'rep', [(i, i ^ bit) for i in range(count)])  36.7 us
    ppermute x71, starting transfers between devices, swap(): return lax.ppermute(value, 'grp', [(i, i ^ flip) for i in range(count)])  33 us
    all_gather x3, waiting for transfers between devices, from_replicas(): whole = lax.all_gather(value, 'rep', axis=1, tiled=True)  32.5 us
    unnamed x104, local copies, waits for them, and re-layouts  17.9 us
  transfers between devices with their start and end apart: 102, of which 50 were waited for; matrix products, arithmetic and copies ran while one was open for 16% of the time, Pallas kernels for 9%

profile of v2, /device:TPU:0, one launch (start us, length us, event | category | flops | bytes accessed | tf_op | source)
XLA Modules:
  0.0 715.6 jit_solution(14451500288630206941)
XLA Ops:
  39.3 10.0 %collective-permute-done.28 = bf16[256,768]{1,0:T(8,128)(2,1)} collective-permute-done((bf16[256,768]{1,0:T(8,128)(2,1)}, bf16[256,768]{1,0:T(8,128)(2,1)}, u32[]{:S(2)}, u32[]{:S(2)}) %collective-permute-start.28) | collective-permute-done | bytes 393248 | tf_op jit(solution)/shard_map/ppermute | solution.py:19
  60.3 11.0 %shard_map.177 = (bf16[1024,768]{1,0:T(8,128)(2,1)}, bf16[1024,256]{1,0:T(8,128)(2,1)}, bf16[1024,1024]{1,0:T(8,128)(2,1)S(1)}) custom-call(s32[1]{0:T(128)} %bitcast.34.me_ref, bf16[1024,1024]{1,0:T(8,128)(2,1)S(1)} %pad_maximum_fusion.5.first_ref, bf16[1024,768]{1,0:T(8,128)(2,1)} %bitcast.327, f32[1,768]{1,0:T(1,128)S(1)} %get-tuple-element.520.bias_ref, ...), custom_call_target="tpu_custom_call" | custom-call | tf_op jit(solution)/shard_map/pallas_call | solution.py:287
  75.9 13.9 %collective-permute-done.35 = bf16[256,1024]{1,0:T(8,128)(2,1)S(1)} collective-permute-done((bf16[256,1024]{1,0:T(8,128)(2,1)S(1)}, bf16[256,1024]{1,0:T(8,128)(2,1)S(1)}, u32[]{:S(2)}, u32[]{:S(2)}) %collective-permute-start.35) | collective-permute-done | bytes 524320 | tf_op jit(solution)/shard_map/ppermute | solution.py:19
  94.4 9.7 %collective-permute-done.37 = bf16[256,1024]{1,0:T(8,128)(2,1)S(1)} collective-permute-done((bf16[256,1024]{1,0:T(8,128)(2,1)S(1)}, bf16[256,1024]{1,0:T(8,128)(2,1)S(1)}, u32[]{:S(2)}, u32[]{:S(2)}) %collective-permute-start.37) | collective-permute-done | bytes 524320 | tf_op jit(solution)/shard_map/ppermute | solution.py:19
  107.5 14.9 %all-gather.4.cloned.1.call-done = bf16[4,256,1024]{2,1,0:T(8,128)(2,1)} async-done(((bf16[4,32,1024]{2,1,0:T(8,128)(2,1)}), bf16[4,256,1024]{2,1,0:T(8,128)(2,1)}) %all-gather.4.cloned.1.call-update) | async-done | bytes 2097168 | tf_op jit(solution)/shard_map/all_gather | solution.py:373
  122.4 10.1 %shard_map.178 = (bf16[1024,1024]{1,0:T(8,128)(2,1)}, bf16[1024,1024]{1,0:T(8,128)(2,1)}, bf16[1024,1024]{1,0:T(8,128)(2,1)S(1)}) custom-call(bf16[1024,1024]{1,0:T(8,128)(2,1)} %pad_maximum_fusion.6.second_ref, bf16[1024,1024]{1,0:T(8,128)(2,1)} %bitcast.341, f32[1,1024]{1,0:T(1,128)S(1)} %get-tuple-element.522.bias_ref, ...), custom_call_target="tpu_custom_call" | custom-call | tf_op jit(solution)/shard_map/pallas_call | solution.py:287
  139.2 12.3 %collective-permute-done.41 = bf16[256,1024]{1,0:T(8,128)(2,1)S(1)} collective-permute-done((bf16[256,1024]{1,0:T(8,128)(2,1)}, bf16[256,1024]{1,0:T(8,128)(2,1)S(1)}, u32[]{:S(2)}, u32[]{:S(2)}) %collective-permute-start.41) | collective-permute-done | bytes 524320 | tf_op jit(solution)/shard_map/ppermute | solution.py:19
  154.8 13.0 %collective-permute-done.43 = bf16[256,1024]{1,0:T(8,128)(2,1)S(1)} collective-permute-done((bf16[256,1024]{1,0:T(8,128)(2,1)S(1)}, bf16[256,1024]{1,0:T(8,128)(2,1)S(1)}, u32[]{:S(2)}, u32[]{:S(2)}) %collective-permute-start.43) | collective-permute-done | bytes 524320 | tf_op jit(solution)/shard_map/ppermute | solution.py:19
  171.2 10.7 %all-gather.6.cloned.1.call-done = bf16[4,256,768]{2,1,0:T(8,128)(2,1)} async-done(((bf16[4,32,768]{2,1,0:T(8,128)(2,1)}), bf16[4,256,768]{2,1,0:T(8,128)(2,1)}) %all-gather.6.cloned.1.call-update) | async-done | bytes 1572880 | tf_op jit(solution)/shard_map/all_gather | solution.py:373
  181.9 10.9 %shard_map.179 = (bf16[1024,768]{1,0:T(8,128)(2,1)}, bf16[1024,256]{1,0:T(8,128)(2,1)}, bf16[1024,1024]{1,0:T(8,128)(2,1)S(1)}) custom-call(s32[1]{0:T(128)} %bitcast.34.me_ref, bf16[1024,1024]{1,0:T(8,128)(2,1)} %pad_maximum_fusion.7.first_ref, bf16[1024,768]{1,0:T(8,128)(2,1)} %bitcast.345, f32[1,768]{1,0:T(1,128)S(1)} %get-tuple-element.519.bias_ref, ...), custom_call_target="tpu_custom_call" | custom-call | tf_op jit(solution)/shard_map/pallas_call | solution.py:287
  199.6 11.4 %collective-permute-done.50 = bf16[256,1024]{1,0:T(8,128)(2,1)S(1)} collective-permute-done((bf16[256,1024]{1,0:T(8,128)(2,1)S(1)}, bf16[256,1024]{1,0:T(8,128)(2,1)S(1)}, u32[]{:S(2)}, u32[]{:S(2)}) %collective-permute-start.50) | collective-permute-done | bytes 524320 | tf_op jit(solution)/shard_map/ppermute | solution.py:19
  222.7 9.9 %collective-permute-done.55 = bf16[256,1024]{1,0:T(8,128)(2,1)S(1)} collective-permute-done((bf16[256,1024]{1,0:T(8,128)(2,1)S(1)}, bf16[256,1024]{1,0:T(8,128)(2,1)S(1)}, u32[]{:S(2)}, u32[]{:S(2)}) %collective-permute-start.55) | collective-permute-done | bytes 524320 | tf_op jit(solution)/shard_map/ppermute | solution.py:19
  270.7 115.5 %conditional.3 = (bf16[1024,1024]{1,0:T(8,128)(2,1)}, bf16[1024,1024]{1,0:T(8,128)(2,1)}, f32[256,1024]{1,0:T(8,128)}, bf16[256,1024]{1,0:T(8,128)(2,1)}, bf16[1...) conditional(s32[]{:T(128)} %convert_element_type.346, () %tuple.65, ...), branch_computations={%region_8.9_spmd, %region_9.24_spmd} | conditional | flops 36959744 | bytes 200989856 | solution.py:496
  278.8 12.2 %collective-permute-done.5 = bf16[256,1024]{1,0:T(8,128)(2,1)S(1)} collective-permute-done((bf16[256,1024]{1,0:T(8,128)(2,1)S(1)}, bf16[256,1024]{1,0:T(8,128)(2,1)S(1)}, u32[]{:S(2)}, u32[]{:S(2)}) %collective-permute-start.5) | collective-permute-done | bytes 524320 | tf_op jit(solution)/shard_map/cond/branch_1_fun/ppermute | solution.py:19
  295.9 11.8 %collective-permute-done.7 = bf16[256,1024]{1,0:T(8,128)(2,1)S(1)} collective-permute-done((bf16[256,1024]{1,0:T(8,128)(2,1)S(1)}, bf16[256,1024]{1,0:T(8,128)(2,1)S(1)}, u32[]{:S(2)}, u32[]{:S(2)}) %collective-permute-start.7) | collective-permute-done | bytes 524320 | tf_op jit(solution)/shard_map/cond/branch_1_fun/ppermute | solution.py:19
  313.7 14.5 %branch_1_fun.7 = (bf16[1024,768]{1,0:T(8,128)(2,1)S(1)}, bf16[1024,1024]{1,0:T(8,128)(2,1)S(1)}, f32[1,768]{1,0:T(1,128)S(1)}) custom-call(s32[1]{0:T(128)} %bitcast.me_ref, bf16[1024,768]{1,0:T(8,128)(2,1)S(1)} %copy-done.58, bf16[1024,1024]{1,0:T(8,128)(2,1)S(1)} %pad_maximum_fusion.branch_ref.refs_2_, ...), custom_call_target="tpu_custom_call" | custom-call | tf_op jit(solution)/shard_map/cond/branch_1_fun/pallas_call | solution.py:287
  340.7 7.8 %collective-permute-done.14 = bf16[256,1024]{1,0:T(8,128)(2,1)S(1)} collective-permute-done((bf16[256,1024]{1,0:T(8,128)(2,1)S(1)}, bf16[256,1024]{1,0:T(8,128)(2,1)S(1)}, u32[]{:S(2)}, u32[]{:S(2)}) %collective-permute-start.14) | collective-permute-done | bytes 524320 | tf_op jit(solution)/shard_map/cond/branch_1_fun/ppermute | solution.py:19
  353.0 12.8 %collective-permute-done.16 = bf16[256,1024]{1,0:T(8,128)(2,1)S(1)} collective-permute-done((bf16[256,1024]{1,0:T(8,128)(2,1)}, bf16[256,1024]{1,0:T(8,128)(2,1)S(1)}, u32[]{:S(2)}, u32[]{:S(2)}) %collective-permute-start.16) | collective-permute-done | bytes 524320 | tf_op jit(solution)/shard_map/cond/branch_1_fun/ppermute | solution.py:19
  398.2 38.5 %conditional.4 = (f32[256,1024]{1,0:T(8,128)}, bf16[1024,1024]{1,0:T(8,128)(2,1)S(1)}, f32[1024]{0:T(1024)S(1)}, f32[1024]{0:T(1024)S(1)}, f32[1024]{0:T(1024)S(...) conditional(s32[]{:T(128)} %convert_element_type.346, () %tuple.73, (f32[256,1024]{1,0:T(8,128)S(1)}, ...), branch_computations={%region_24.25_spmd, %region_25.34_spmd} | conditional | flops 17559808 | bytes 32558380 | solution.py:496
  403.5 13.2 %collective-permute-done.20 = bf16[256,1024]{1,0:T(8,128)(2,1)S(1)} collective-permute-done((bf16[256,1024]{1,0:T(8,128)(2,1)S(1)}, bf16[256,1024]{1,0:T(8,128)(2,1)S(1)}, u32[]{:S(2)}, u32[]{:S(2)}) %collective-permute-start.20) | collective-permute-done | bytes 524320 | tf_op jit(solution)/shard_map/cond/branch_1_fun/ppermute | solution.py:19
  421.7 12.7 %collective-permute-done.22 = bf16[256,1024]{1,0:T(8,128)(2,1)S(1)} collective-permute-done((bf16[256,1024]{1,0:T(8,128)(2,1)S(1)}, bf16[256,1024]{1,0:T(8,128)(2,1)S(1)}, u32[]{:S(2)}, u32[]{:S(2)}) %collective-permute-start.22) | collective-permute-done | bytes 524320 | tf_op jit(solution)/shard_map/cond/branch_1_fun/ppermute | solution.py:19
  442.1 48.3 %conditional.5 = (bf16[1024,1024]{1,0:T(8,128)(2,1)}, f32[1,6,1024]{2,1,0:T(8,128)S(1)}, f32[1,1536]{1,0:T(1,128)S(1)}, f32[1,256,1024]{2,1,0:T(8,128)}) conditional(s32[]{:T(128)} %convert_element_type.346, () %tuple.72, (s32[]{:T(128)}, bf16[2,256,1024]{2,1,0:T(8,128)(2,1)}, bf16[1024,768]{1,0:T(8,128)(2,1)}, bf16[1024,1024]{1,0:T(8,128)(2,1)S(1)}, ...), branch_computations={%region_36.37_spmd, %region_37.44_spmd} | conditional | flops 7865600 | bytes 43113712 | solution.py:496
  443.5 17.0 %branch_1_fun.12 = (bf16[1024,768]{1,0:T(8,128)(2,1)S(1)}, bf16[1024,1024]{1,0:T(8,128)(2,1)S(1)}, f32[1,768]{1,0:T(1,128)S(1)}) custom-call(s32[1]{0:T(128)} %bitcast.19.me_ref, bf16[1024,768]{1,0:T(8,128)(2,1)} %get-tuple-element.134.mixed_ref, bf16[1024,1024]{1,0:T(8,128)(2,1)} %copy-done.25, bf16[256,1024]{1,0:T(8,128)(2,1)S(1)} %slice_bitcast_fusion.2.back_ref, ...), custom_call_target="tpu_custom_call" | custom-call | tf_op jit(solution)/shard_map/cond/branch_1_fun/pallas_call | solution.py:287
  472.9 13.0 %collective-permute-done.2 = bf16[256,1024]{1,0:T(8,128)(2,1)S(1)} collective-permute-done((bf16[256,1024]{1,0:T(8,128)(2,1)S(1)}, bf16[256,1024]{1,0:T(8,128)(2,1)S(1)}, u32[]{:S(2)}, u32[]{:S(2)}) %collective-permute-start.2) | collective-permute-done | bytes 524320 | tf_op jit(solution)/shard_map/cond/branch_1_fun/ppermute | solution.py:19
  515.6 16.0 %collective-permute-done.90 = bf16[1,128,1024]{2,1,0:T(8,128)(2,1)S(1)} collective-permute-done((bf16[1,128,1024]{2,1,0:T(8,128)(2,1)S(1)}, bf16[1,128,1024]{2,1,0:T(8,128)(2,1)S(1)}, u32[]{:S(2)}, u32[]{:S(2)}) %collective-permute-start.90) | collective-permute-done | bytes 262176 | tf_op jit(solution)/shard_map/ppermute | solution.py:61
  538.3 18.2 %collective-permute-done.71 = bf16[1,128,1024]{2,1,0:T(8,128)(2,1)S(1)} collective-permute-done((bf16[1,128,1024]{2,1,0:T(8,128)(2,1)S(1)}, bf16[1,128,1024]{2,1,0:T(8,128)(2,1)S(1)}, u32[]{:S(2)}, u32[]{:S(2)}) %collective-permute-start.71) | collective-permute-done | bytes 262176 | tf_op jit(solution)/shard_map/ppermute | solution.py:61
  578.1 9.9 %collective-permute-done.75 = bf16[1,128,1024]{2,1,0:T(8,128)(2,1)S(1)} collective-permute-done((bf16[1,128,1024]{2,1,0:T(8,128)(2,1)S(1)}, bf16[1,128,1024]{2,1,0:T(8,128)(2,1)S(1)}, u32[]{:S(2)}, u32[]{:S(2)}) %collective-permute-start.75) | collective-permute-done | bytes 262176 | tf_op jit(solution)/shard_map/ppermute | solution.py:61
  592.1 10.3 %collective-permute-done.96 = f32[24576]{0:T(1024)S(1)} collective-permute-done((f32[24576]{0:T(1024)S(1)}, f32[24576]{0:T(1024)S(1)}, u32[]{:S(2)}, u32[]{:S(2)}) %collective-permute-start.96) | collective-permute-done | bytes 98336 | tf_op jit(solution)/shard_map/ppermute | solution.py:61
  618.0 8.3 %collective-permute-done.63 = bf16[1,128,1024]{2,1,0:T(8,128)(2,1)} collective-permute-done((bf16[1,128,1024]{2,1,0:T(8,128)(2,1)}, bf16[1,128,1024]{2,1,0:T(8,128)(2,1)}, u32[]{:S(2)}, u32[]{:S(2)}) %collective-permute-start.63) | collective-permute-done | bytes 262176 | tf_op jit(solution)/shard_map/ppermute | solution.py:61
  638.9 10.2 %collective-permute-done.67 = bf16[1,128,1024]{2,1,0:T(8,128)(2,1)S(1)} collective-permute-done((bf16[1,128,1024]{2,1,0:T(8,128)(2,1)S(1)}, bf16[1,128,1024]{2,1,0:T(8,128)(2,1)S(1)}, u32[]{:S(2)}, u32[]{:S(2)}) %collective-permute-start.67) | collective-permute-done | bytes 262176 | tf_op jit(solution)/shard_map/ppermute | solution.py:61
  666.4 11.2 %collective-permute-done.85 = bf16[4,128,1024]{2,1,0:T(8,128)(2,1)S(1)} collective-permute-done((bf16[4,128,1024]{2,1,0:T(8,128)(2,1)S(1)}, bf16[4,128,1024]{2,1,0:T(8,128)(2,1)S(1)}, u32[]{:S(2)}, u32[]{:S(2)}) %collective-permute-start.85) | collective-permute-done | bytes 1048608 | tf_op jit(solution)/shard_map/ppermute | solution.py:61
  682.2 17.4 %collective-permute-done.69 = bf16[4,128,1024]{2,1,0:T(8,128)(2,1)S(1)} collective-permute-done((bf16[4,128,1024]{2,1,0:T(8,128)(2,1)S(1)}, bf16[4,128,1024]{2,1,0:T(8,128)(2,1)S(1)}, u32[]{:S(2)}, u32[]{:S(2)}) %collective-permute-start.69) | collective-permute-done | bytes 1048608 | tf_op jit(solution)/shard_map/ppermute | solution.py:61
  (594 shorter events, 344.9 us)
Async XLA Ops:
  7.2 115.2 %all-gather.4.cloned.1.call-start = ((), (), s32[]{:S(2)}) async-start(), calls=%async_computation | async-start | bytes 2359296 | tf_op jit(solution)/shard_map/all_gather | solution.py:373
  18.9 20.2 %collective-permute-start.25 = (bf16[256,1024]{1,0:T(8,128)(2,1)}, bf16[256,1024]{1,0:T(8,128)(2,1)}, u32[]{:S(2)}, u32[]{:S(2)}) collective-permute-start(bf16[256,1024]{1,0:T(8,128)(2,1)} %add_convert_fusion.11), channel_id=1, source_target_pairs={{0,16},{8,24},{16,0},{24,8},{1,17},{9,25},{17,1},{25,9},{2,18},{10... | collective-permute-start | bytes 1572872 | tf_op jit(solution)/shard_map/ppermute | solution.py:19
  20.8 37.4 %collective-permute-start.24 = (bf16[256,1024]{1,0:T(8,128)(2,1)}, bf16[256,1024]{1,0:T(8,128)(2,1)}, u32[]{:S(2)}, u32[]{:S(2)}) collective-permute-start(bf16[256,1024]{1,0:T(8,128)(2,1)} %add_convert_fusion.11), channel_id=1, source_target_pairs={{0,8},{8,0},{16,24},{24,16},{1,9},{9,1},{17,25},{25,17},{2,10},{10... | collective-permute-start | bytes 1572872 | tf_op jit(solution)/shard_map/ppermute | solution.py:19
  39.1 19.1 %collective-permute-start.26 = (bf16[256,1024]{1,0:T(8,128)(2,1)}, bf16[256,1024]{1,0:T(8,128)(2,1)S(1)}, u32[]{:S(2)}, u32[]{:S(2)}) collective-permute-start(bf16[256,1024]{1,0:T(8,128)(2,1)} %collective-permute-done.25), channel_id=1, source_target_pairs={{0,8},{8,0},{16,24},{24,16},{1,9},{9,1},{17,25},{25,17},{2,10},{10... | collective-permute-start | bytes 1572872 | tf_op jit(solution)/shard_map/ppermute | solution.py:19
  72.5 109.4 %all-gather.6.cloned.1.call-start = ((), (), s32[]{:S(2)}) async-start(), calls=%async_computation.1 | async-start | bytes 1769472 | tf_op jit(solution)/shard_map/all_gather | solution.py:373
  104.2 30.8 %collective-permute-start.46 = (bf16[32,1792]{1,0:T(8,128)(2,1)S(1)}, bf16[32,1792]{1,0:T(8,128)(2,1)}, u32[]{:S(2)}, u32[]{:S(2)}) collective-permute-start(bf16[32,1792]{1,0:T(8,128)(2,1)S(1)} %get-tuple-element.467), channel_id=1, source_target_pairs={{0,16},{8,24},{16,0},{24,8},{1,17},{9,25},{17,1},{25,9},{2,18},{10... | collective-permute-start | bytes 344072 | tf_op jit(solution)/shard_map/ppermute | solution.py:19
  138.9 104.0 %all-gather.8.cloned.1.call-start = ((), (), s32[]{:S(2)}) async-start(), calls=%async_computation.2 | async-start | bytes 2359296 | tf_op jit(solution)/shard_map/all_gather | solution.py:373
  194.6 242.1 %all-reduce.3.cloned.1.call-start = ((), (), s32[]{:S(2)}) async-start(), calls=%async_computation.3 | async-start | bytes 8388608 | tf_op jit(solution)/shard_map/psum | solution.py:508
  198.9 23.2 %collective-permute-start.52 = (bf16[256,1024]{1,0:T(8,128)(2,1)S(1)}, bf16[256,1024]{1,0:T(8,128)(2,1)S(1)}, u32[]{:S(2)}, u32[]{:S(2)}) collective-permute-start(bf16[256,1024]{1,0:T(8,128)(2,1)S(1)} %bitcast_convert_fusion), channel_id=1, source_target_pairs={{0,16},{8,24},{16,0},{24,8},{1,17},{9,25},{17,1},{25,9},{2,18},{10... | collective-permute-start | bytes 1572872 | tf_op jit(solution)/shard_map/ppermute | solution.py:19
  213.1 19.5 %collective-permute-start.55 = (bf16[256,1024]{1,0:T(8,128)(2,1)S(1)}, bf16[256,1024]{1,0:T(8,128)(2,1)S(1)}, u32[]{:S(2)}, u32[]{:S(2)}) collective-permute-start(bf16[256,1024]{1,0:T(8,128)(2,1)S(1)} %add_convert_fusion.5), channel_id=1, source_target_pairs={{0,16},{8,24},{16,0},{24,8},{1,17},{9,25},{17,1},{25,9},{2,18},{10... | collective-permute-start | bytes 1572872 | tf_op jit(solution)/shard_map/ppermute | solution.py:19
  388.4 48.3 %collective-permute-start.57 = (bf16[4,128,1024]{2,1,0:T(8,128)(2,1)}, bf16[4,128,1024]{2,1,0:T(8,128)(2,1)}, u32[]{:S(2)}, u32[]{:S(2)}) collective-permute-start(bf16[4,128,1024]{2,1,0:T(8,128)(2,1)} %dynamic-slice_bitcast_fusion.3), channel_id=1, source_target_pairs={{0,1},{1,0},{2,3},{3,2},{4,5},{5,4},{6,7},{7,6},{8,9},{9,8},{10,11... | collective-permute-start | bytes 3145736 | tf_op jit(solution)/shard_map/ppermute | solution.py:61
  392.0 99.7 %collective-permute-start.59 = (bf16[4,128,1024]{2,1,0:T(8,128)(2,1)}, bf16[4,128,1024]{2,1,0:T(8,128)(2,1)}, u32[]{:S(2)}, u32[]{:S(2)}) collective-permute-start(bf16[4,128,1024]{2,1,0:T(8,128)(2,1)} %dynamic-slice_bitcast_fusion.2), channel_id=1, source_target_pairs={{0,1},{1,0},{2,3},{3,2},{4,5},{5,4},{6,7},{7,6},{8,9},{9,8},{10,11... | collective-permute-start | bytes 3145736 | tf_op jit(solution)/shard_map/ppermute | solution.py:61
  397.6 94.1 %collective-permute-start.60 = (bf16[4,128,1024]{2,1,0:T(8,128)(2,1)}, bf16[4,128,1024]{2,1,0:T(8,128)(2,1)}, u32[]{:S(2)}, u32[]{:S(2)}) collective-permute-start(bf16[4,128,1024]{2,1,0:T(8,128)(2,1)} %dynamic-slice_bitcast_fusion.1), channel_id=1, source_target_pairs={{0,1},{1,0},{2,3},{3,2},{4,5},{5,4},{6,7},{7,6},{8,9},{9,8},{10,11... | collective-permute-start | bytes 3145736 | tf_op jit(solution)/shard_map/ppermute | solution.py:61
  440.6 51.1 %collective-permute-start.58 = (bf16[2,128,1024]{2,1,0:T(8,128)(2,1)}, bf16[2,128,1024]{2,1,0:T(8,128)(2,1)}, u32[]{:S(2)}, u32[]{:S(2)}) collective-permute-start(bf16[2,128,1024]{2,1,0:T(8,128)(2,1)} %dynamic-slice_bitcast_fusion.10), channel_id=1, source_target_pairs={{0,2},{1,3},{2,0},{3,1},{4,6},{5,7},{6,4},{7,5},{8,10},{9,11},{10,... | collective-permute-start | bytes 1572872 | tf_op jit(solution)/shard_map/ppermute | solution.py:61
  493.8 21.3 %collective-permute-start.78 = (bf16[2,128,1024]{2,1,0:T(8,128)(2,1)S(1)}, bf16[2,128,1024]{2,1,0:T(8,128)(2,1)S(1)}, u32[]{:S(2)}, u32[]{:S(2)}) collective-permute-start(bf16[2,128,1024]{2,1,0:T(8,128)(2,1)S(1)} %dynamic-slice_bitcast_fusion.7), channel_id=1, source_target_pairs={{0,2},{1,3},{2,0},{3,1},{4,6},{5,7},{6,4},{7,5},{8,10},{9,11},{10,... | collective-permute-start | bytes 1572872 | tf_op jit(solution)/shard_map/ppermute | solution.py:61
  497.8 37.4 %collective-permute-start.87 = (bf16[256,1024]{1,0:T(8,128)(2,1)S(1)}, bf16[256,1024]{1,0:T(8,128)(2,1)S(1)}, u32[]{:S(2)}, u32[]{:S(2)}) collective-permute-start(bf16[256,1024]{1,0:T(8,128)(2,1)S(1)} %get-tuple-element.397), channel_id=1, source_target_pairs={{0,16},{8,24},{16,0},{24,8},{1,17},{9,25},{17,1},{25,9},{2,18},{10... | collective-permute-start | bytes 1572872 | tf_op jit(solution)/shard_map/ppermute | solution.py:19
  498.4 36.9 %collective-permute-start.88 = (bf16[256,1024]{1,0:T(8,128)(2,1)S(1)}, bf16[256,1024]{1,0:T(8,128)(2,1)S(1)}, u32[]{:S(2)}, u32[]{:S(2)}) collective-permute-start(bf16[256,1024]{1,0:T(8,128)(2,1)S(1)} %get-tuple-element.396), channel_id=1, source_target_pairs={{0,24},{8,16},{16,8},{24,0},{1,25},{9,17},{17,9},{25,1},{2,26},{10... | collective-permute-start | bytes 1572872 | tf_op jit(solution)/shard_map/ppermute | solution.py:19
  501.1 73.0 %collective-permute-start.61 = (bf16[4,128,1024]{2,1,0:T(8,128)(2,1)S(1)}, bf16[4,128,1024]{2,1,0:T(8,128)(2,1)S(1)}, u32[]{:S(2)}, u32[]{:S(2)}) collective-permute-start(bf16[4,128,1024]{2,1,0:T(8,128)(2,1)S(1)} %dynamic-slice_bitcast_fusion), channel_id=1, source_target_pairs={{0,1},{1,0},{2,3},{3,2},{4,5},{5,4},{6,7},{7,6},{8,9},{9,8},{10,11... | collective-permute-start | bytes 3145736 | tf_op jit(solution)/shard_map/ppermute | solution.py:61
  511.9 23.7 %collective-permute-start.70 = (bf16[2,128,1024]{2,1,0:T(8,128)(2,1)S(1)}, bf16[2,128,1024]{2,1,0:T(8,128)(2,1)S(1)}, u32[]{:S(2)}, u32[]{:S(2)}) collective-permute-start(bf16[2,128,1024]{2,1,0:T(8,128)(2,1)S(1)} %dynamic-slice_bitcast_fusion.8), channel_id=1, source_target_pairs={{0,2},{1,3},{2,0},{3,1},{4,6},{5,7},{6,4},{7,5},{8,10},{9,11},{10,... | collective-permute-start | bytes 1572872 | tf_op jit(solution)/shard_map/ppermute | solution.py:61
  531.7 24.9 %collective-permute-start.79 = (bf16[1,128,1024]{2,1,0:T(8,128)(2,1)S(1)}, bf16[1,128,1024]{2,1,0:T(8,128)(2,1)S(1)}, u32[]{:S(2)}, u32[]{:S(2)}) collective-permute-start(bf16[1,128,1024]{2,1,0:T(8,128)(2,1)S(1)} %constant_dynamic-slice_fusion.5), channel_id=1, source_target_pairs={{0,4},{1,5},{2,6},{3,7},{4,0},{5,1},{6,2},{7,3},{8,12},{9,13},{10,... | collective-permute-start | bytes 786440 | tf_op jit(solution)/shard_map/ppermute | solution.py:61
  535.2 36.9 %collective-permute-start.91 = (bf16[2,128,1024]{2,1,0:T(8,128)(2,1)S(1)}, bf16[2,128,1024]{2,1,0:T(8,128)(2,1)S(1)}, u32[]{:S(2)}, u32[]{:S(2)}) collective-permute-start(bf16[2,128,1024]{2,1,0:T(8,128)(2,1)S(1)} %pad_maximum_fusion.24), channel_id=1, source_target_pairs={{0,2},{1,3},{2,0},{3,1},{4,6},{5,7},{6,4},{7,5},{8,10},{9,11},{10,... | collective-permute-start | bytes 1572872 | tf_op jit(solution)/shard_map/ppermute | solution.py:61
  535.8 20.7 %collective-permute-start.71 = (bf16[1,128,1024]{2,1,0:T(8,128)(2,1)S(1)}, bf16[1,128,1024]{2,1,0:T(8,128)(2,1)S(1)}, u32[]{:S(2)}, u32[]{:S(2)}) collective-permute-start(bf16[1,128,1024]{2,1,0:T(8,128)(2,1)S(1)} %constant_dynamic-slice_fusion.6), channel_id=1, source_target_pairs={{0,4},{1,5},{2,6},{3,7},{4,0},{5,1},{6,2},{7,3},{8,12},{9,13},{10,... | collective-permute-start | bytes 786440 | tf_op jit(solution)/shard_map/ppermute | solution.py:61
  567.3 20.7 %collective-permute-start.75 = (bf16[1,128,1024]{2,1,0:T(8,128)(2,1)S(1)}, bf16[1,128,1024]{2,1,0:T(8,128)(2,1)S(1)}, u32[]{:S(2)}, u32[]{:S(2)}) collective-permute-start(bf16[1,128,1024]{2,1,0:T(8,128)(2,1)S(1)} %maximum_bitcast_fusion.7), channel_id=1, source_target_pairs={{0,4},{1,5},{2,6},{3,7},{4,0},{5,1},{6,2},{7,3},{8,12},{9,13},{10,... | collective-permute-start | bytes 786440 | tf_op jit(solution)/shard_map/ppermute | solution.py:61
  570.7 21.3 %collective-permute-start.83 = (bf16[1,128,1024]{2,1,0:T(8,128)(2,1)S(1)}, bf16[1,128,1024]{2,1,0:T(8,128)(2,1)S(1)}, u32[]{:S(2)}, u32[]{:S(2)}) collective-permute-start(bf16[1,128,1024]{2,1,0:T(8,128)(2,1)S(1)} %bitcast.397), channel_id=1, source_target_pairs={{0,4},{1,5},{2,6},{3,7},{4,0},{5,1},{6,2},{7,3},{8,12},{9,13},{10,... | collective-permute-start | bytes 786440 | tf_op jit(solution)/shard_map/ppermute | solution.py:61
  573.2 76.2 %collective-permute-start.92 = (bf16[4,128,1024]{2,1,0:T(8,128)(2,1)}, bf16[4,128,1024]{2,1,0:T(8,128)(2,1)}, u32[]{:S(2)}, u32[]{:S(2)}) collective-permute-start(bf16[4,128,1024]{2,1,0:T(8,128)(2,1)} %pad_maximum_fusion.20), channel_id=1, source_target_pairs={{0,1},{1,0},{2,3},{3,2},{4,5},{5,4},{6,7},{7,6},{8,9},{9,8},{10,11... | collective-permute-start | bytes 3145736 | tf_op jit(solution)/shard_map/ppermute | solution.py:61
  575.4 34.4 %collective-permute-start.62 = (bf16[2,128,1024]{2,1,0:T(8,128)(2,1)}, bf16[2,128,1024]{2,1,0:T(8,128)(2,1)}, u32[]{:S(2)}, u32[]{:S(2)}) collective-permute-start(bf16[2,128,1024]{2,1,0:T(8,128)(2,1)} %dynamic-slice_bitcast_fusion.9), channel_id=1, source_target_pairs={{0,2},{1,3},{2,0},{3,1},{4,6},{5,7},{6,4},{7,5},{8,10},{9,11},{10,... | collective-permute-start | bytes 1572872 | tf_op jit(solution)/shard_map/ppermute | solution.py:61
  577.6 24.8 %collective-permute-start.96 = (f32[24576]{0:T(1024)S(1)}, f32[24576]{0:T(1024)S(1)}, u32[]{:S(2)}, u32[]{:S(2)}) collective-permute-start(f32[24576]{0:T(1024)S(1)} %add.471), channel_id=1, source_target_pairs={{0,2},{1,3},{2,0},{3,1},{4,6},{5,7},{6,4},{7,5},{8,10},{9,11},{10,... | collective-permute-start | bytes 294920 | tf_op jit(solution)/shard_map/ppermute | solution.py:61
  589.1 38.4 %collective-permute-start.76 = (bf16[2,128,1024]{2,1,0:T(8,128)(2,1)}, bf16[2,128,1024]{2,1,0:T(8,128)(2,1)}, u32[]{:S(2)}, u32[]{:S(2)}) collective-permute-start(bf16[2,128,1024]{2,1,0:T(8,128)(2,1)} %pad_maximum_fusion.22), channel_id=1, source_target_pairs={{0,2},{1,3},{2,0},{3,1},{4,6},{5,7},{6,4},{7,5},{8,10},{9,11},{10,... | collective-permute-start | bytes 1572872 | tf_op jit(solution)/shard_map/ppermute | solution.py:61
  603.4 33.4 %collective-permute-start.84 = (bf16[2,128,1024]{2,1,0:T(8,128)(2,1)}, bf16[2,128,1024]{2,1,0:T(8,128)(2,1)}, u32[]{:S(2)}, u32[]{:S(2)}) collective-permute-start(bf16[2,128,1024]{2,1,0:T(8,128)(2,1)} %pad_maximum_fusion.23), channel_id=1, source_target_pairs={{0,2},{1,3},{2,0},{3,1},{4,6},{5,7},{6,4},{7,5},{8,10},{9,11},{10,... | collective-permute-start | bytes 1572872 | tf_op jit(solution)/shard_map/ppermute | solution.py:61
  629.0 35.3 %collective-permute-start.77 = (bf16[4,128,1024]{2,1,0:T(8,128)(2,1)S(1)}, bf16[4,128,1024]{2,1,0:T(8,128)(2,1)S(1)}, u32[]{:S(2)}, u32[]{:S(2)}) collective-permute-start(bf16[4,128,1024]{2,1,0:T(8,128)(2,1)S(1)} %pad_maximum_fusion.18), channel_id=1, source_target_pairs={{0,1},{1,0},{2,3},{3,2},{4,5},{5,4},{6,7},{7,6},{8,9},{9,8},{10,11... | collective-permute-start | bytes 3145736 | tf_op jit(solution)/shard_map/ppermute | solution.py:61
  638.0 39.5 %collective-permute-start.85 = (bf16[4,128,1024]{2,1,0:T(8,128)(2,1)S(1)}, bf16[4,128,1024]{2,1,0:T(8,128)(2,1)S(1)}, u32[]{:S(2)}, u32[]{:S(2)}) collective-permute-start(bf16[4,128,1024]{2,1,0:T(8,128)(2,1)S(1)} %pad_maximum_fusion.19), channel_id=1, source_target_pairs={{0,1},{1,0},{2,3},{3,2},{4,5},{5,4},{6,7},{7,6},{8,9},{9,8},{10,11... | collective-permute-start | bytes 3145736 | tf_op jit(solution)/shard_map/ppermute | solution.py:61
  663.1 36.5 %collective-permute-start.69 = (bf16[4,128,1024]{2,1,0:T(8,128)(2,1)S(1)}, bf16[4,128,1024]{2,1,0:T(8,128)(2,1)S(1)}, u32[]{:S(2)}, u32[]{:S(2)}) collective-permute-start(bf16[4,128,1024]{2,1,0:T(8,128)(2,1)S(1)} %pad_maximum_fusion.17), channel_id=1, source_target_pairs={{0,1},{1,0},{2,3},{3,2},{4,5},{5,4},{6,7},{7,6},{8,9},{9,8},{10,11... | collective-permute-start | bytes 3145736 | tf_op jit(solution)/shard_map/ppermute | solution.py:61
  (133 other events, 982.7 us)
Sparse Core Ops, SparseCore 0:
  72.6 49.7 all-gather.3
  139.1 42.7 all-gather.5
  194.7 48.1 all-gather.7
  269.0 155.1 all-reduce.2

commit v3 on v2

--- a/solution.py
+++ b/solution.py
@@ -23,6 +23,11 @@
     far = swap(block, 2)
     near = swap(block, 1)
     return jnp.concatenate([block, near, far, swap(far, 1)], 0)
+
+
+def spread_rounds(block):
+    (far,) = yield [swap(block, 2)]
+    return jnp.concatenate([block, swap(block, 1), far, swap(far, 1)], 0)
 
 
 def collect(parts):
@@ -345,6 +350,9 @@
     me = lax.axis_index("grp")
     replica = lax.axis_index("rep")
 
+    small = jnp.concatenate([norm_gain, norm_shift, branch_bias[:, 2:]], 1)
+    small = lax.all_gather(small, "grp", axis=2, tiled=True).astype(F32)
+
     def columns_by_device(weight, pieces):
         wide = weight.shape[1] // pieces
         size = wide // groups
@@ -373,60 +381,87 @@
         whole = lax.all_gather(value, "rep", axis=1, tiled=True)
         return whole.reshape(width, value.shape[-1])
 
-    sent = slices_by_device(expand[0], 1)
+    sent = slices_by_device(tied([expand[0]], small)[0], 1)
     slice_up = at_once(exchange(sent, me))
     up_columns[0] = from_replicas(slice_up)
     sent = columns_by_device(tied([project_in[0]], sent)[0], 3)
     in_columns[0] = at_once(exchange(sent, me)).reshape(width, 3 * part)
     in_columns[0] = tied([in_columns[0]], slice_up)[0]
-    slices = []
-    for index in range(1, layers):
-        pair = [slices_by_device(project_in[index], 3), slices_by_device(expand[index], 1)]
-        both = at_once(exchange(tied([jnp.concatenate(pair, -1)], sent)[0], me))
-        slices.append((both[..., : 3 * part], both[..., 3 * part :]))
-
-    small = jnp.concatenate([norm_gain, norm_shift, branch_bias[:, 2:]], 1)
-    small = lax.all_gather(small, "grp", axis=2, tiled=True).astype(F32)
     gains, shifts, out_biases = small[:, 0:2], small[:, 2:4], small[:, 4:6]
     mix_bias = jnp.concatenate(
         [branch_bias[:, 0], jnp.zeros_like(branch_bias[:, 0]), branch_bias[:, 1]], -1
     ).astype(F32)
     up_bias = expand_bias.astype(F32)
 
+    def segment(run):
+        shapes = jax.eval_shape(run)
+        return lax.cond(
+            replica < 4 * replicas,
+            run,
+            lambda: jax.tree.map(lambda leaf: jnp.zeros(leaf.shape, leaf.dtype), shapes),
+        )
+
+    def start_both(index, g_both):
+        rounds.add("both %d" % index, replica_sum(by_replica(g_both), turn_both, bits))
+
     state = inputs[0]
     saved = []
+    hat, _ = normed(state)
+    first = spread((hat * gains[0, 0] + shifts[0, 0]).astype(BF16))
+    length = first.shape[0]
+    rounds = Rounds()
+    for index in range(1, layers):
+        pair = [slices_by_device(project_in[index], 3), slices_by_device(expand[index], 1)]
+        rounds.add(index, exchange(tied([jnp.concatenate(pair, -1)], sent)[0], me))
+    cotangent_own = cotangent[0].astype(BF16)
+    rounds.add("cotangent", spread_rounds(cotangent_own))
     for index in range(layers):
-        hat, _ = normed(state)
-        first = spread((hat * gains[index, 0] + shifts[index, 0]).astype(BF16))
-        length = first.shape[0]
-        mixed, attended, branch = kernel_call(
-            attend_kernel,
-            [first, in_columns[index], mix_bias[index : index + 1], project_out[index]],
-            [((length, 3 * part), BF16), ((length, part), BF16), ((length, width), BF16)],
-            me=me,
-            head=head,
-            blocks=groups,
-        )
+
+        def attend():
+            mixed, attended, branch = kernel_call(
+                attend_kernel,
+                [first, in_columns[index], mix_bias[index : index + 1], project_out[index]],
+                [((length, 3 * part), BF16), ((length, part), BF16), ((length, width), BF16)],
+                me=me,
+                head=head,
+                blocks=groups,
+            )
+            middle = state + collect(branch) + out_biases[index, 0]
+            hat, _ = normed(middle)
+            second = spread((hat * gains[index, 1] + shifts[index, 1]).astype(BF16))
+            return mixed, attended, middle, second
+
+        def feed():
+            return kernel_call(
+                feed_kernel,
+                [second, up_columns[index], up_bias[index : index + 1], contract[index]],
+                [((length, hidden_part), BF16)] * 2 + [((length, width), BF16)],
+                blocks=groups,
+            )
+
+        def feed_on():
+            active, slope, down = feed()
+            state = middle + collect(down) + out_biases[index, 1]
+            hat, _ = normed(state)
+            following = (hat * gains[index + 1, 0] + shifts[index + 1, 0]).astype(BF16)
+            return active, slope, state, spread(following)
+
+        before = state, first
+        if index:
+            mixed, attended, middle, second = attend()
+        else:
+            mixed, attended, middle, second = segment(attend)
+            second = rounds.meet(second, *rounds.going)
         if index < layers - 1:
-            in_columns[index + 1] = from_replicas(tied([slices[index][0]], attended)[0])
-        middle = state + collect(branch) + out_biases[index, 0]
-        hat, _ = normed(middle)
-        second = spread((hat * gains[index, 1] + shifts[index, 1]).astype(BF16))
-        active, slope, down = kernel_call(
-            feed_kernel,
-            [second, up_columns[index], up_bias[index : index + 1], contract[index]],
-            [((length, hidden_part), BF16)] * 2 + [((length, width), BF16)],
-            blocks=groups,
-        )
-        if index < layers - 1:
-            up_columns[index + 1] = from_replicas(tied([slices[index][1]], active)[0])
-            state_after = middle + collect(down) + out_biases[index, 1]
-        saved.append((state, first, mixed, attended, middle, second, slope, active, down))
-        if index < layers - 1:
-            state = state_after
-
-
-    rounds = Rounds()
+            down = None
+            moved = rounds.done[index + 1]
+            in_columns[index + 1] = from_replicas(moved[..., : 3 * part])
+            active, slope, state, first = feed_on()
+            up_columns[index + 1] = from_replicas(tied([moved[..., 3 * part :]], active)[0])
+        else:
+            active, slope, down = feed()
+        saved.append((*before, mixed, attended, middle, second, slope, active, down))
+
 
     def by_replica(value):
         cut = value.reshape(groups, replicas, slice_rows, value.shape[1])
@@ -441,10 +476,11 @@
         return jnp.concatenate([turned, value[:, 3 * part :]], 1)
 
     bits = replica_bits()
-    def feed_back(index, grad):
+    def feed_back(index, grad, d_down=None):
         second, slope, active = saved[index][5:8]
         d_down_own = grad.astype(BF16)
-        d_down = spread(d_down_own)
+        if d_down is None:
+            d_down = spread(d_down_own)
         d_raised, partial, d_up_bias = kernel_call(
             feed_back_kernel,
             [d_down, slope, contract[index], up_columns[index]],
@@ -491,20 +527,9 @@
         own_part = jnp.concatenate([d_mix_bias[0, :part], d_mix_bias[0, 2 * part :], d_up_bias[0]])
         return g_both, (own_rows, own_part), d_middle + d_first, state
 
-    def segment(run):
-        shapes = jax.eval_shape(run)
-        return lax.cond(
-            replica < 4 * replicas,
-            run,
-            lambda: jax.tree.map(lambda leaf: jnp.zeros(leaf.shape, leaf.dtype), shapes),
-        )
-
-    def start_both(index, g_both):
-        rounds.add("both %d" % index, replica_sum(by_replica(g_both), turn_both, bits))
-
     last = layers - 1
     small = [None] * layers
-    g_contract, g_expand, kept = feed_back(last, cotangent[0])
+    g_contract, g_expand, kept = feed_back(last, cotangent[0], rounds.done["cotangent"])
     beside = lax.psum((g_contract, g_expand), "rep")
 
     def first_segment():

time: 726 us -> 735 us (1.012)
  local copies, waits for them, and re-layouts: 70.3 us -> 78.8 us
    unnamed x104 -> x128, local copies, waits for them, and re-layouts: 17.9 us -> 21.3 us
  transfers between devices with their start and end apart: 102 -> 102, of which waited for: 50 -> 48; matrix products, arithmetic and copies ran while one was open for 16% -> 18% of each run, Pallas kernels for 9% -> 9%
where the time goes in v3:
time: 735 us; the launch traced here: 725 us
  waiting for transfers between devices  355 us (48%)
  Pallas kernels  108 us (15%)
  other arithmetic  86.6 us (12%)
  local copies, waits for them, and re-layouts  78.8 us (11%)
  starting transfers between devices  74.4 us (10%)
  between operations  15.8 us (2%)
    ppermute x71, waiting for transfers between devices, swap(): return lax.ppermute(value, 'grp', [(i, i ^ flip) for i in range(count)])  204 us
    ppermute x27, waiting for transfers between devices, cross(): return lax.ppermute(value, 'rep', [(i, i ^ bit) for i in range(count)])  123 us
    pallas_call x14, Pallas kernels, kernel_call(): pl.pallas_call(functools.partial(kernel, **sizes), out_shape=[jax.ShapeDt...  108 us
    ppermute x71, starting transfers between devices, swap(): return lax.ppermute(value, 'grp', [(i, i ^ flip) for i in range(count)])  37.4 us
    ppermute x27, starting transfers between devices, cross(): return lax.ppermute(value, 'rep', [(i, i ^ bit) for i in range(count)])  36.5 us
    all_gather x3, waiting for transfers between devices, from_replicas(): whole = lax.all_gather(value, 'rep', axis=1, tiled=True)  27.9 us
    unnamed x128, local copies, waits for them, and re-layouts  21.3 us
  transfers between devices with their start and end apart: 102, of which 48 were waited for; matrix products, arithmetic and copies ran while one was open for 18% of the time, Pallas kernels for 9%

profile of v3, /device:TPU:0, one launch (start us, length us, event | category | flops | bytes accessed | tf_op | source)
XLA Modules:
  0.0 725.2 jit_solution(2472832761080235780)
XLA Ops:
  47.6 9.5 %collective-permute-done.34 = bf16[256,768]{1,0:T(8,128)(2,1)} collective-permute-done((bf16[256,768]{1,0:T(8,128)(2,1)}, bf16[256,768]{1,0:T(8,128)(2,1)}, u32[]{:S(2)}, u32[]{:S(2)}) %collective-permute-start.34) | collective-permute-done | bytes 393248 | tf_op jit(solution)/shard_map/ppermute | solution.py:19
  71.0 44.2 %conditional.4 = (bf16[1024,768]{1,0:T(8,128)(2,1)S(1)}, bf16[1024,256]{1,0:T(8,128)(2,1)S(1)}, f32[256,1024]{1,0:T(8,128)}, bf16[1024,1024]{1,0:T(8,128)(2,1)S(1)}) conditional(s32[]{:T(128)} %convert_element_type.348, () %tuple.75, (s32[]{:T(128)}, f32[2,768]{1,0:T(2,128)S(1)}, bf16[2,256,1024]{2,1,0:T(8,128)(2,1)S(1)}, ...), branch_computations={%region_2.3_spmd, %region_3.6_spmd} | conditional | flops 13631744 | bytes 27839760 | solution.py:398
  83.2 12.5 %collective-permute-done.5 = bf16[256,1024]{1,0:T(8,128)(2,1)S(1)} collective-permute-done((bf16[256,1024]{1,0:T(8,128)(2,1)S(1)}, bf16[256,1024]{1,0:T(8,128)(2,1)S(1)}, u32[]{:S(2)}, u32[]{:S(2)}) %collective-permute-start.5) | collective-permute-done | bytes 524320 | tf_op jit(solution)/shard_map/cond/branch_1_fun/ppermute | solution.py:19
  100.6 12.4 %collective-permute-done.7 = bf16[256,1024]{1,0:T(8,128)(2,1)S(1)} collective-permute-done((bf16[256,1024]{1,0:T(8,128)(2,1)S(1)}, bf16[256,1024]{1,0:T(8,128)(2,1)S(1)}, u32[]{:S(2)}, u32[]{:S(2)}) %collective-permute-start.7) | collective-permute-done | bytes 524320 | tf_op jit(solution)/shard_map/cond/branch_1_fun/ppermute | solution.py:19
  120.7 8.8 %collective-permute-done.42 = bf16[256,1024]{1,0:T(8,128)(2,1)S(1)} collective-permute-done((bf16[256,1024]{1,0:T(8,128)(2,1)}, bf16[256,1024]{1,0:T(8,128)(2,1)S(1)}, u32[]{:S(2)}, u32[]{:S(2)}) %collective-permute-start.42) | collective-permute-done | bytes 524320 | tf_op jit(solution)/shard_map/ppermute | solution.py:19
  129.5 10.7 %shard_map.177 = (bf16[1024,1024]{1,0:T(8,128)(2,1)}, bf16[1024,1024]{1,0:T(8,128)(2,1)}, bf16[1024,1024]{1,0:T(8,128)(2,1)S(1)}) custom-call(bf16[1024,1024]{1,0:T(8,128)(2,1)} %copy-done.21, bf16[1024,1024]{1,0:T(8,128)(2,1)} %bitcast.341, f32[1,1024]{1,0:T(1,128)S(1)} %get-tuple-element.559.bias_ref, bf16[1024,1024]{1,0:T(8,128)(2,1)S(1)} %get-tuple-element.423.down_ref), custom_call_target="tpu_custom_call" | custom-call | tf_op jit(solution)/shard_map/pallas_call | solution.py:292
  145.9 12.1 %collective-permute-done.45 = bf16[256,1024]{1,0:T(8,128)(2,1)S(1)} collective-permute-done((bf16[256,1024]{1,0:T(8,128)(2,1)S(1)}, bf16[256,1024]{1,0:T(8,128)(2,1)S(1)}, u32[]{:S(2)}, u32[]{:S(2)}) %collective-permute-start.45) | collective-permute-done | bytes 524320 | tf_op jit(solution)/shard_map/ppermute | solution.py:19
  161.1 12.8 %collective-permute-done.47 = bf16[256,1024]{1,0:T(8,128)(2,1)S(1)} collective-permute-done((bf16[256,1024]{1,0:T(8,128)(2,1)S(1)}, bf16[256,1024]{1,0:T(8,128)(2,1)S(1)}, u32[]{:S(2)}, u32[]{:S(2)}) %collective-permute-start.47) | collective-permute-done | bytes 524320 | tf_op jit(solution)/shard_map/ppermute | solution.py:19
  177.3 14.1 %all-gather.6.cloned.1.call-done = bf16[4,256,768]{2,1,0:T(8,128)(2,1)} async-done(((bf16[4,32,768]{2,1,0:T(8,128)(2,1)}), bf16[4,256,768]{2,1,0:T(8,128)(2,1)}) %all-gather.6.cloned.1.call-update) | async-done | bytes 1572880 | tf_op jit(solution)/shard_map/all_gather | solution.py:381
  191.3 10.9 %shard_map.178 = (bf16[1024,768]{1,0:T(8,128)(2,1)}, bf16[1024,256]{1,0:T(8,128)(2,1)}, bf16[1024,1024]{1,0:T(8,128)(2,1)S(1)}) custom-call(s32[1]{0:T(128)} %bitcast.83.me_ref, bf16[1024,1024]{1,0:T(8,128)(2,1)} %pad_maximum_fusion.7.first_ref, bf16[1024,768]{1,0:T(8,128)(2,1)} %bitcast.345, f32[1,768]{1,0:T(1,128)S(1)} %slice.730.bias_ref, ...), custom_call_target="tpu_custom_call" | custom-call | tf_op jit(solution)/shard_map/pallas_call | solution.py:292
  208.4 12.5 %collective-permute-done.51 = bf16[256,1024]{1,0:T(8,128)(2,1)S(1)} collective-permute-done((bf16[256,1024]{1,0:T(8,128)(2,1)S(1)}, bf16[256,1024]{1,0:T(8,128)(2,1)S(1)}, u32[]{:S(2)}, u32[]{:S(2)}) %collective-permute-start.51) | collective-permute-done | bytes 524320 | tf_op jit(solution)/shard_map/ppermute | solution.py:19
  223.9 11.3 %collective-permute-done.55 = bf16[256,1024]{1,0:T(8,128)(2,1)S(1)} collective-permute-done((bf16[256,1024]{1,0:T(8,128)(2,1)S(1)}, bf16[256,1024]{1,0:T(8,128)(2,1)S(1)}, u32[]{:S(2)}, u32[]{:S(2)}) %collective-permute-start.55) | collective-permute-done | bytes 524320 | tf_op jit(solution)/shard_map/ppermute | solution.py:19
  238.6 13.9 %all-gather.8.cloned.1.call-done = bf16[4,256,1024]{2,1,0:T(8,128)(2,1)} async-done(((bf16[4,32,1024]{2,1,0:T(8,128)(2,1)}), bf16[4,256,1024]{2,1,0:T(8,128)(2,1)}) %all-gather.8.cloned.1.call-update) | async-done | bytes 2097168 | tf_op jit(solution)/shard_map/all_gather | solution.py:381
  280.0 115.5 %conditional.5 = (bf16[1024,1024]{1,0:T(8,128)(2,1)}, bf16[1024,1024]{1,0:T(8,128)(2,1)}, f32[256,1024]{1,0:T(8,128)}, bf16[256,1024]{1,0:T(8,128)(2,1)}, bf16[1...) conditional(s32[]{:T(128)} %convert_element_type.348, () %tuple.74, ...), branch_computations={%region_10.11_spmd, %region_11.26_spmd} | conditional | flops 36959744 | bytes 198892672 | solution.py:398
  288.1 12.2 %collective-permute-done.11 = bf16[256,1024]{1,0:T(8,128)(2,1)S(1)} collective-permute-done((bf16[256,1024]{1,0:T(8,128)(2,1)S(1)}, bf16[256,1024]{1,0:T(8,128)(2,1)S(1)}, u32[]{:S(2)}, u32[]{:S(2)}) %collective-permute-start.11) | collective-permute-done | bytes 524320 | tf_op jit(solution)/shard_map/cond/branch_1_fun/ppermute | solution.py:19
  305.2 11.8 %collective-permute-done.13 = bf16[256,1024]{1,0:T(8,128)(2,1)S(1)} collective-permute-done((bf16[256,1024]{1,0:T(8,128)(2,1)S(1)}, bf16[256,1024]{1,0:T(8,128)(2,1)S(1)}, u32[]{:S(2)}, u32[]{:S(2)}) %collective-permute-start.13) | collective-permute-done | bytes 524320 | tf_op jit(solution)/shard_map/cond/branch_1_fun/ppermute | solution.py:19
  323.0 14.7 %branch_1_fun.9 = (bf16[1024,768]{1,0:T(8,128)(2,1)S(1)}, bf16[1024,1024]{1,0:T(8,128)(2,1)S(1)}, f32[1,768]{1,0:T(1,128)S(1)}) custom-call(s32[1]{0:T(128)} %bitcast.5.me_ref, bf16[1024,768]{1,0:T(8,128)(2,1)S(1)} %copy-done.61, bf16[1024,1024]{1,0:T(8,128)(2,1)S(1)} %pad_maximum_fusion.1.branch_ref.refs_2_, ...), custom_call_target="tpu_custom_call" | custom-call | tf_op jit(solution)/shard_map/cond/branch_1_fun/pallas_call | solution.py:292
  362.1 12.8 %collective-permute-done.22 = bf16[256,1024]{1,0:T(8,128)(2,1)S(1)} collective-permute-done((bf16[256,1024]{1,0:T(8,128)(2,1)}, bf16[256,1024]{1,0:T(8,128)(2,1)S(1)}, u32[]{:S(2)}, u32[]{:S(2)}) %collective-permute-start.22) | collective-permute-done | bytes 524320 | tf_op jit(solution)/shard_map/cond/branch_1_fun/ppermute | solution.py:19
  407.4 39.0 %conditional.6 = (f32[256,1024]{1,0:T(8,128)S(1)}, bf16[1024,1024]{1,0:T(8,128)(2,1)S(1)}, f32[1024]{0:T(1024)S(1)}, f32[1024]{0:T(1024)S(1)}, f32[1024]{0:T(102...) conditional(s32[]{:T(128)} %convert_element_type.348, () %tuple.85, (f32[256,1024]{1,0:T(8,128)}, ...), branch_computations={%region_26.27_spmd, %region_27.36_spmd} | conditional | flops 17559808 | bytes 32558380 | solution.py:398
  414.1 11.9 %collective-permute-done.26 = bf16[256,1024]{1,0:T(8,128)(2,1)S(1)} collective-permute-done((bf16[256,1024]{1,0:T(8,128)(2,1)S(1)}, bf16[256,1024]{1,0:T(8,128)(2,1)S(1)}, u32[]{:S(2)}, u32[]{:S(2)}) %collective-permute-start.26) | collective-permute-done | bytes 524320 | tf_op jit(solution)/shard_map/cond/branch_1_fun/ppermute | solution.py:19
  431.7 12.7 %collective-permute-done.28 = bf16[256,1024]{1,0:T(8,128)(2,1)S(1)} collective-permute-done((bf16[256,1024]{1,0:T(8,128)(2,1)S(1)}, bf16[256,1024]{1,0:T(8,128)(2,1)S(1)}, u32[]{:S(2)}, u32[]{:S(2)}) %collective-permute-start.28) | collective-permute-done | bytes 524320 | tf_op jit(solution)/shard_map/cond/branch_1_fun/ppermute | solution.py:19
  453.4 46.8 %conditional.7 = (bf16[1024,1024]{1,0:T(8,128)(2,1)}, f32[1,6,1024]{2,1,0:T(8,128)S(1)}, f32[1,1536]{1,0:T(1,128)S(1)}, f32[1,256,1024]{2,1,0:T(8,128)}) conditional(s32[]{:T(128)} %convert_element_type.348, () %tuple.84, (s32[]{:T(128)}, bf16[2,256,1024]{2,1,0:T(8,128)(2,1)S(1)}, bf16[1024,768]{1,0:T(8,128)(2,1)}, bf16[1024,1024]{1,0:T(8,128)(2,1)}, ...), branch_computations={%region_38.39_spmd, %region_39.46_spmd} | conditional | flops 7865600 | bytes 43113740 | solution.py:398
  454.4 17.1 %branch_1_fun.14 = (bf16[1024,768]{1,0:T(8,128)(2,1)S(1)}, bf16[1024,1024]{1,0:T(8,128)(2,1)S(1)}, f32[1,768]{1,0:T(1,128)S(1)}) custom-call(s32[1]{0:T(128)} %bitcast.24.me_ref, bf16[1024,768]{1,0:T(8,128)(2,1)} %get-tuple-element.164.mixed_ref, bf16[1024,1024]{1,0:T(8,128)(2,1)} %get-tuple-element.165.branch_ref.refs_2_, ...), custom_call_target="tpu_custom_call" | custom-call | tf_op jit(solution)/shard_map/cond/branch_1_fun/pallas_call | solution.py:292
  484.0 13.0 %collective-permute-done.2 = bf16[256,1024]{1,0:T(8,128)(2,1)S(1)} collective-permute-done((bf16[256,1024]{1,0:T(8,128)(2,1)S(1)}, bf16[256,1024]{1,0:T(8,128)(2,1)S(1)}, u32[]{:S(2)}, u32[]{:S(2)}) %collective-permute-start.2) | collective-permute-done | bytes 524320 | tf_op jit(solution)/shard_map/cond/branch_1_fun/ppermute | solution.py:19
  525.5 16.0 %collective-permute-done.90 = bf16[1,128,1024]{2,1,0:T(8,128)(2,1)S(1)} collective-permute-done((bf16[1,128,1024]{2,1,0:T(8,128)(2,1)S(1)}, bf16[1,128,1024]{2,1,0:T(8,128)(2,1)S(1)}, u32[]{:S(2)}, u32[]{:S(2)}) %collective-permute-start.90) | collective-permute-done | bytes 262176 | tf_op jit(solution)/shard_map/ppermute | solution.py:66
  548.1 18.2 %collective-permute-done.71 = bf16[1,128,1024]{2,1,0:T(8,128)(2,1)S(1)} collective-permute-done((bf16[1,128,1024]{2,1,0:T(8,128)(2,1)S(1)}, bf16[1,128,1024]{2,1,0:T(8,128)(2,1)S(1)}, u32[]{:S(2)}, u32[]{:S(2)}) %collective-permute-start.71) | collective-permute-done | bytes 262176 | tf_op jit(solution)/shard_map/ppermute | solution.py:66
  587.7 10.1 %collective-permute-done.75 = bf16[1,128,1024]{2,1,0:T(8,128)(2,1)S(1)} collective-permute-done((bf16[1,128,1024]{2,1,0:T(8,128)(2,1)S(1)}, bf16[1,128,1024]{2,1,0:T(8,128)(2,1)S(1)}, u32[]{:S(2)}, u32[]{:S(2)}) %collective-permute-start.75) | collective-permute-done | bytes 262176 | tf_op jit(solution)/shard_map/ppermute | solution.py:66
  601.9 10.3 %collective-permute-done.96 = f32[24576]{0:T(1024)S(1)} collective-permute-done((f32[24576]{0:T(1024)S(1)}, f32[24576]{0:T(1024)S(1)}, u32[]{:S(2)}, u32[]{:S(2)}) %collective-permute-start.96) | collective-permute-done | bytes 98336 | tf_op jit(solution)/shard_map/ppermute | solution.py:66
  627.8 8.3 %collective-permute-done.63 = bf16[1,128,1024]{2,1,0:T(8,128)(2,1)} collective-permute-done((bf16[1,128,1024]{2,1,0:T(8,128)(2,1)}, bf16[1,128,1024]{2,1,0:T(8,128)(2,1)}, u32[]{:S(2)}, u32[]{:S(2)}) %collective-permute-start.63) | collective-permute-done | bytes 262176 | tf_op jit(solution)/shard_map/ppermute | solution.py:66
  648.8 10.2 %collective-permute-done.67 = bf16[1,128,1024]{2,1,0:T(8,128)(2,1)S(1)} collective-permute-done((bf16[1,128,1024]{2,1,0:T(8,128)(2,1)S(1)}, bf16[1,128,1024]{2,1,0:T(8,128)(2,1)S(1)}, u32[]{:S(2)}, u32[]{:S(2)}) %collective-permute-start.67) | collective-permute-done | bytes 262176 | tf_op jit(solution)/shard_map/ppermute | solution.py:66
  676.2 11.2 %collective-permute-done.85 = bf16[4,128,1024]{2,1,0:T(8,128)(2,1)S(1)} collective-permute-done((bf16[4,128,1024]{2,1,0:T(8,128)(2,1)S(1)}, bf16[4,128,1024]{2,1,0:T(8,128)(2,1)S(1)}, u32[]{:S(2)}, u32[]{:S(2)}) %collective-permute-start.85) | collective-permute-done | bytes 1048608 | tf_op jit(solution)/shard_map/ppermute | solution.py:66
  692.0 17.4 %collective-permute-done.69 = bf16[4,128,1024]{2,1,0:T(8,128)(2,1)S(1)} collective-permute-done((bf16[4,128,1024]{2,1,0:T(8,128)(2,1)S(1)}, bf16[4,128,1024]{2,1,0:T(8,128)(2,1)S(1)}, u32[]{:S(2)}, u32[]{:S(2)}) %collective-permute-start.69) | collective-permute-done | bytes 1048608 | tf_op jit(solution)/shard_map/ppermute | solution.py:66
  (622 shorter events, 359.6 us)
Async XLA Ops:
  7.2 122.3 %all-gather.4.cloned.1.call-start = ((), (), s32[]{:S(2)}) async-start(), calls=%async_computation | async-start | bytes 2359296 | tf_op jit(solution)/shard_map/all_gather | solution.py:381
  19.5 27.1 %collective-permute-start.31 = (bf16[256,1024]{1,0:T(8,128)(2,1)}, bf16[256,1024]{1,0:T(8,128)(2,1)}, u32[]{:S(2)}, u32[]{:S(2)}) collective-permute-start(bf16[256,1024]{1,0:T(8,128)(2,1)} %add_convert_fusion.11), channel_id=1, source_target_pairs={{0,16},{8,24},{16,0},{24,8},{1,17},{9,25},{17,1},{25,9},{2,18},{10... | collective-permute-start | bytes 1572872 | tf_op jit(solution)/shard_map/ppermute | solution.py:19
  21.4 46.1 %collective-permute-start.30 = (bf16[256,1024]{1,0:T(8,128)(2,1)}, bf16[256,1024]{1,0:T(8,128)(2,1)}, u32[]{:S(2)}, u32[]{:S(2)}) collective-permute-start(bf16[256,1024]{1,0:T(8,128)(2,1)} %add_convert_fusion.11), channel_id=1, source_target_pairs={{0,8},{8,0},{16,24},{24,16},{1,9},{9,1},{17,25},{25,17},{2,10},{10... | collective-permute-start | bytes 1572872 | tf_op jit(solution)/shard_map/ppermute | solution.py:19
  39.4 151.9 %all-gather.6.cloned.1.call-start = ((), (), s32[]{:S(2)}) async-start(), calls=%async_computation.1 | async-start | bytes 1769472 | tf_op jit(solution)/shard_map/all_gather | solution.py:381
  41.3 79.4 %collective-permute-start.39 = (bf16[32,1792]{1,0:T(8,128)(2,1)}, bf16[32,1792]{1,0:T(8,128)(2,1)}, u32[]{:S(2)}, u32[]{:S(2)}) collective-permute-start(bf16[32,1792]{1,0:T(8,128)(2,1)} %get-tuple-element.512), channel_id=1, source_target_pairs={{0,8},{8,0},{16,24},{24,16},{1,9},{9,1},{17,25},{25,17},{2,10},{10... | collective-permute-start | bytes 344072 | tf_op jit(solution)/shard_map/ppermute | solution.py:19
  46.6 21.0 %collective-permute-start.32 = (bf16[256,1024]{1,0:T(8,128)(2,1)}, bf16[256,1024]{1,0:T(8,128)(2,1)S(1)}, u32[]{:S(2)}, u32[]{:S(2)}) collective-permute-start(bf16[256,1024]{1,0:T(8,128)(2,1)} %collective-permute-done.31), channel_id=1, source_target_pairs={{0,8},{8,0},{16,24},{24,16},{1,9},{9,1},{17,25},{25,17},{2,10},{10... | collective-permute-start | bytes 1572872 | tf_op jit(solution)/shard_map/ppermute | solution.py:19
  57.1 63.6 %collective-permute-start.40 = (bf16[32,1792]{1,0:T(8,128)(2,1)}, bf16[32,1792]{1,0:T(8,128)(2,1)}, u32[]{:S(2)}, u32[]{:S(2)}) collective-permute-start(bf16[32,1792]{1,0:T(8,128)(2,1)} %get-tuple-element.511), channel_id=1, source_target_pairs={{0,16},{8,24},{16,0},{24,8},{1,17},{9,25},{17,1},{25,9},{2,18},{10... | collective-permute-start | bytes 344072 | tf_op jit(solution)/shard_map/ppermute | solution.py:19
  64.4 56.3 %collective-permute-start.41 = (bf16[32,1792]{1,0:T(8,128)(2,1)}, bf16[32,1792]{1,0:T(8,128)(2,1)S(1)}, u32[]{:S(2)}, u32[]{:S(2)}) collective-permute-start(bf16[32,1792]{1,0:T(8,128)(2,1)} %get-tuple-element.510), channel_id=1, source_target_pairs={{0,24},{8,16},{16,8},{24,0},{1,25},{9,17},{17,9},{25,1},{2,26},{10... | collective-permute-start | bytes 344072 | tf_op jit(solution)/shard_map/ppermute | solution.py:19
  145.9 106.6 %all-gather.8.cloned.1.call-start = ((), (), s32[]{:S(2)}) async-start(), calls=%async_computation.2 | async-start | bytes 2359296 | tf_op jit(solution)/shard_map/all_gather | solution.py:381
  204.1 242.3 %all-reduce.3.cloned.1.call-start = ((), (), s32[]{:S(2)}) async-start(), calls=%async_computation.3 | async-start | bytes 8388608 | tf_op jit(solution)/shard_map/psum | solution.py:533
  397.7 50.0 %collective-permute-start.57 = (bf16[4,128,1024]{2,1,0:T(8,128)(2,1)}, bf16[4,128,1024]{2,1,0:T(8,128)(2,1)}, u32[]{:S(2)}, u32[]{:S(2)}) collective-permute-start(bf16[4,128,1024]{2,1,0:T(8,128)(2,1)} %dynamic-slice_bitcast_fusion.3), channel_id=1, source_target_pairs={{0,1},{1,0},{2,3},{3,2},{4,5},{5,4},{6,7},{7,6},{8,9},{9,8},{10,11... | collective-permute-start | bytes 3145736 | tf_op jit(solution)/shard_map/ppermute | solution.py:66
  401.3 100.3 %collective-permute-start.59 = (bf16[4,128,1024]{2,1,0:T(8,128)(2,1)}, bf16[4,128,1024]{2,1,0:T(8,128)(2,1)}, u32[]{:S(2)}, u32[]{:S(2)}) collective-permute-start(bf16[4,128,1024]{2,1,0:T(8,128)(2,1)} %dynamic-slice_bitcast_fusion.2), channel_id=1, source_target_pairs={{0,1},{1,0},{2,3},{3,2},{4,5},{5,4},{6,7},{7,6},{8,9},{9,8},{10,11... | collective-permute-start | bytes 3145736 | tf_op jit(solution)/shard_map/ppermute | solution.py:66
  406.9 94.7 %collective-permute-start.60 = (bf16[4,128,1024]{2,1,0:T(8,128)(2,1)}, bf16[4,128,1024]{2,1,0:T(8,128)(2,1)}, u32[]{:S(2)}, u32[]{:S(2)}) collective-permute-start(bf16[4,128,1024]{2,1,0:T(8,128)(2,1)} %dynamic-slice_bitcast_fusion.1), channel_id=1, source_target_pairs={{0,1},{1,0},{2,3},{3,2},{4,5},{5,4},{6,7},{7,6},{8,9},{9,8},{10,11... | collective-permute-start | bytes 3145736 | tf_op jit(solution)/shard_map/ppermute | solution.py:66
  451.9 49.7 %collective-permute-start.58 = (bf16[2,128,1024]{2,1,0:T(8,128)(2,1)}, bf16[2,128,1024]{2,1,0:T(8,128)(2,1)}, u32[]{:S(2)}, u32[]{:S(2)}) collective-permute-start(bf16[2,128,1024]{2,1,0:T(8,128)(2,1)} %dynamic-slice_bitcast_fusion.10), channel_id=1, source_target_pairs={{0,2},{1,3},{2,0},{3,1},{4,6},{5,7},{6,4},{7,5},{8,10},{9,11},{10,... | collective-permute-start | bytes 1572872 | tf_op jit(solution)/shard_map/ppermute | solution.py:66
  503.7 21.2 %collective-permute-start.78 = (bf16[2,128,1024]{2,1,0:T(8,128)(2,1)S(1)}, bf16[2,128,1024]{2,1,0:T(8,128)(2,1)S(1)}, u32[]{:S(2)}, u32[]{:S(2)}) collective-permute-start(bf16[2,128,1024]{2,1,0:T(8,128)(2,1)S(1)} %dynamic-slice_bitcast_fusion.7), channel_id=1, source_target_pairs={{0,2},{1,3},{2,0},{3,1},{4,6},{5,7},{6,4},{7,5},{8,10},{9,11},{10,... | collective-permute-start | bytes 1572872 | tf_op jit(solution)/shard_map/ppermute | solution.py:66
  507.6 37.4 %collective-permute-start.87 = (bf16[256,1024]{1,0:T(8,128)(2,1)S(1)}, bf16[256,1024]{1,0:T(8,128)(2,1)S(1)}, u32[]{:S(2)}, u32[]{:S(2)}) collective-permute-start(bf16[256,1024]{1,0:T(8,128)(2,1)S(1)} %get-tuple-element.441), channel_id=1, source_target_pairs={{0,16},{8,24},{16,0},{24,8},{1,17},{9,25},{17,1},{25,9},{2,18},{10... | collective-permute-start | bytes 1572872 | tf_op jit(solution)/shard_map/ppermute | solution.py:19
  508.2 36.9 %collective-permute-start.88 = (bf16[256,1024]{1,0:T(8,128)(2,1)S(1)}, bf16[256,1024]{1,0:T(8,128)(2,1)S(1)}, u32[]{:S(2)}, u32[]{:S(2)}) collective-permute-start(bf16[256,1024]{1,0:T(8,128)(2,1)S(1)} %get-tuple-element.440), channel_id=1, source_target_pairs={{0,24},{8,16},{16,8},{24,0},{1,25},{9,17},{17,9},{25,1},{2,26},{10... | collective-permute-start | bytes 1572872 | tf_op jit(solution)/shard_map/ppermute | solution.py:19
  510.9 73.0 %collective-permute-start.61 = (bf16[4,128,1024]{2,1,0:T(8,128)(2,1)S(1)}, bf16[4,128,1024]{2,1,0:T(8,128)(2,1)S(1)}, u32[]{:S(2)}, u32[]{:S(2)}) collective-permute-start(bf16[4,128,1024]{2,1,0:T(8,128)(2,1)S(1)} %dynamic-slice_bitcast_fusion), channel_id=1, source_target_pairs={{0,1},{1,0},{2,3},{3,2},{4,5},{5,4},{6,7},{7,6},{8,9},{9,8},{10,11... | collective-permute-start | bytes 3145736 | tf_op jit(solution)/shard_map/ppermute | solution.py:66
  521.7 23.7 %collective-permute-start.70 = (bf16[2,128,1024]{2,1,0:T(8,128)(2,1)S(1)}, bf16[2,128,1024]{2,1,0:T(8,128)(2,1)S(1)}, u32[]{:S(2)}, u32[]{:S(2)}) collective-permute-start(bf16[2,128,1024]{2,1,0:T(8,128)(2,1)S(1)} %dynamic-slice_bitcast_fusion.8), channel_id=1, source_target_pairs={{0,2},{1,3},{2,0},{3,1},{4,6},{5,7},{6,4},{7,5},{8,10},{9,11},{10,... | collective-permute-start | bytes 1572872 | tf_op jit(solution)/shard_map/ppermute | solution.py:66
  541.5 24.9 %collective-permute-start.79 = (bf16[1,128,1024]{2,1,0:T(8,128)(2,1)S(1)}, bf16[1,128,1024]{2,1,0:T(8,128)(2,1)S(1)}, u32[]{:S(2)}, u32[]{:S(2)}) collective-permute-start(bf16[1,128,1024]{2,1,0:T(8,128)(2,1)S(1)} %constant_dynamic-slice_fusion.5), channel_id=1, source_target_pairs={{0,4},{1,5},{2,6},{3,7},{4,0},{5,1},{6,2},{7,3},{8,12},{9,13},{10,... | collective-permute-start | bytes 786440 | tf_op jit(solution)/shard_map/ppermute | solution.py:66
  545.0 36.9 %collective-permute-start.91 = (bf16[2,128,1024]{2,1,0:T(8,128)(2,1)S(1)}, bf16[2,128,1024]{2,1,0:T(8,128)(2,1)S(1)}, u32[]{:S(2)}, u32[]{:S(2)}) collective-permute-start(bf16[2,128,1024]{2,1,0:T(8,128)(2,1)S(1)} %pad_maximum_fusion.24), channel_id=1, source_target_pairs={{0,2},{1,3},{2,0},{3,1},{4,6},{5,7},{6,4},{7,5},{8,10},{9,11},{10,... | collective-permute-start | bytes 1572872 | tf_op jit(solution)/shard_map/ppermute | solution.py:66
  545.6 20.7 %collective-permute-start.71 = (bf16[1,128,1024]{2,1,0:T(8,128)(2,1)S(1)}, bf16[1,128,1024]{2,1,0:T(8,128)(2,1)S(1)}, u32[]{:S(2)}, u32[]{:S(2)}) collective-permute-start(bf16[1,128,1024]{2,1,0:T(8,128)(2,1)S(1)} %constant_dynamic-slice_fusion.6), channel_id=1, source_target_pairs={{0,4},{1,5},{2,6},{3,7},{4,0},{5,1},{6,2},{7,3},{8,12},{9,13},{10,... | collective-permute-start | bytes 786440 | tf_op jit(solution)/shard_map/ppermute | solution.py:66
  577.1 20.7 %collective-permute-start.75 = (bf16[1,128,1024]{2,1,0:T(8,128)(2,1)S(1)}, bf16[1,128,1024]{2,1,0:T(8,128)(2,1)S(1)}, u32[]{:S(2)}, u32[]{:S(2)}) collective-permute-start(bf16[1,128,1024]{2,1,0:T(8,128)(2,1)S(1)} %maximum_bitcast_fusion.7), channel_id=1, source_target_pairs={{0,4},{1,5},{2,6},{3,7},{4,0},{5,1},{6,2},{7,3},{8,12},{9,13},{10,... | collective-permute-start | bytes 786440 | tf_op jit(solution)/shard_map/ppermute | solution.py:66
  580.5 21.3 %collective-permute-start.83 = (bf16[1,128,1024]{2,1,0:T(8,128)(2,1)S(1)}, bf16[1,128,1024]{2,1,0:T(8,128)(2,1)S(1)}, u32[]{:S(2)}, u32[]{:S(2)}) collective-permute-start(bf16[1,128,1024]{2,1,0:T(8,128)(2,1)S(1)} %bitcast.397), channel_id=1, source_target_pairs={{0,4},{1,5},{2,6},{3,7},{4,0},{5,1},{6,2},{7,3},{8,12},{9,13},{10,... | collective-permute-start | bytes 786440 | tf_op jit(solution)/shard_map/ppermute | solution.py:66
  583.0 76.2 %collective-permute-start.92 = (bf16[4,128,1024]{2,1,0:T(8,128)(2,1)}, bf16[4,128,1024]{2,1,0:T(8,128)(2,1)}, u32[]{:S(2)}, u32[]{:S(2)}) collective-permute-start(bf16[4,128,1024]{2,1,0:T(8,128)(2,1)} %pad_maximum_fusion.20), channel_id=1, source_target_pairs={{0,1},{1,0},{2,3},{3,2},{4,5},{5,4},{6,7},{7,6},{8,9},{9,8},{10,11... | collective-permute-start | bytes 3145736 | tf_op jit(solution)/shard_map/ppermute | solution.py:66
  585.2 34.4 %collective-permute-start.62 = (bf16[2,128,1024]{2,1,0:T(8,128)(2,1)}, bf16[2,128,1024]{2,1,0:T(8,128)(2,1)}, u32[]{:S(2)}, u32[]{:S(2)}) collective-permute-start(bf16[2,128,1024]{2,1,0:T(8,128)(2,1)} %dynamic-slice_bitcast_fusion.9), channel_id=1, source_target_pairs={{0,2},{1,3},{2,0},{3,1},{4,6},{5,7},{6,4},{7,5},{8,10},{9,11},{10,... | collective-permute-start | bytes 1572872 | tf_op jit(solution)/shard_map/ppermute | solution.py:66
  587.5 24.7 %collective-permute-start.96 = (f32[24576]{0:T(1024)S(1)}, f32[24576]{0:T(1024)S(1)}, u32[]{:S(2)}, u32[]{:S(2)}) collective-permute-start(f32[24576]{0:T(1024)S(1)} %add.460), channel_id=1, source_target_pairs={{0,2},{1,3},{2,0},{3,1},{4,6},{5,7},{6,4},{7,5},{8,10},{9,11},{10,... | collective-permute-start | bytes 294920 | tf_op jit(solution)/shard_map/ppermute | solution.py:66
  599.0 38.3 %collective-permute-start.76 = (bf16[2,128,1024]{2,1,0:T(8,128)(2,1)}, bf16[2,128,1024]{2,1,0:T(8,128)(2,1)}, u32[]{:S(2)}, u32[]{:S(2)}) collective-permute-start(bf16[2,128,1024]{2,1,0:T(8,128)(2,1)} %pad_maximum_fusion.22), channel_id=1, source_target_pairs={{0,2},{1,3},{2,0},{3,1},{4,6},{5,7},{6,4},{7,5},{8,10},{9,11},{10,... | collective-permute-start | bytes 1572872 | tf_op jit(solution)/shard_map/ppermute | solution.py:66
  613.2 33.4 %collective-permute-start.84 = (bf16[2,128,1024]{2,1,0:T(8,128)(2,1)}, bf16[2,128,1024]{2,1,0:T(8,128)(2,1)}, u32[]{:S(2)}, u32[]{:S(2)}) collective-permute-start(bf16[2,128,1024]{2,1,0:T(8,128)(2,1)} %pad_maximum_fusion.23), channel_id=1, source_target_pairs={{0,2},{1,3},{2,0},{3,1},{4,6},{5,7},{6,4},{7,5},{8,10},{9,11},{10,... | collective-permute-start | bytes 1572872 | tf_op jit(solution)/shard_map/ppermute | solution.py:66
  638.9 35.3 %collective-permute-start.77 = (bf16[4,128,1024]{2,1,0:T(8,128)(2,1)S(1)}, bf16[4,128,1024]{2,1,0:T(8,128)(2,1)S(1)}, u32[]{:S(2)}, u32[]{:S(2)}) collective-permute-start(bf16[4,128,1024]{2,1,0:T(8,128)(2,1)S(1)} %pad_maximum_fusion.18), channel_id=1, source_target_pairs={{0,1},{1,0},{2,3},{3,2},{4,5},{5,4},{6,7},{7,6},{8,9},{9,8},{10,11... | collective-permute-start | bytes 3145736 | tf_op jit(solution)/shard_map/ppermute | solution.py:66
  647.9 39.5 %collective-permute-start.85 = (bf16[4,128,1024]{2,1,0:T(8,128)(2,1)S(1)}, bf16[4,128,1024]{2,1,0:T(8,128)(2,1)S(1)}, u32[]{:S(2)}, u32[]{:S(2)}) collective-permute-start(bf16[4,128,1024]{2,1,0:T(8,128)(2,1)S(1)} %pad_maximum_fusion.19), channel_id=1, source_target_pairs={{0,1},{1,0},{2,3},{3,2},{4,5},{5,4},{6,7},{7,6},{8,9},{9,8},{10,11... | collective-permute-start | bytes 3145736 | tf_op jit(solution)/shard_map/ppermute | solution.py:66
  672.9 36.5 %collective-permute-start.69 = (bf16[4,128,1024]{2,1,0:T(8,128)(2,1)S(1)}, bf16[4,128,1024]{2,1,0:T(8,128)(2,1)S(1)}, u32[]{:S(2)}, u32[]{:S(2)}) collective-permute-start(bf16[4,128,1024]{2,1,0:T(8,128)(2,1)S(1)} %pad_maximum_fusion.17), channel_id=1, source_target_pairs={{0,1},{1,0},{2,3},{3,2},{4,5},{5,4},{6,7},{7,6},{8,9},{9,8},{10,11... | collective-permute-start | bytes 3145736 | tf_op jit(solution)/shard_map/ppermute | solution.py:66
  (145 other events, 1019.6 us)
Sparse Core Ops, SparseCore 0:
  39.5 50.5 all-gather.3
  146.0 45.3 all-gather.5
  204.3 48.1 all-gather.7
  278.6 155.1 all-reduce.2
